TPU v7x, 512 devices: a whole 4x8x8 slice. The times are simulated.
512 devices in a mesh: outer: 128 (over z, y, core), inner: 4 (over x).
Axes of the slice: x: 4, y: 8, z: 8, core: 2. Of those that a mesh axis runs over, the one named last changes fastest.
Arguments:
- query_states: bfloat16 [65536, 4096], P(('outer', 'inner')), may hold values from -6 to 6
- key_states: bfloat16 [65536, 4096], P(('outer', 'inner')), may hold values from -6 to 6
- value_states: bfloat16 [65536, 4096], P(('outer', 'inner')), may hold values from -6 to 6
- doc_lengths: int32 [128], replicated, may hold values from 1 to 1024, 65536 in all
- slopes: float32 [32], replicated, may hold values from 0.00024414062 to 0.0625
Outputs:
- attended: bfloat16 [65536, 4096], P(('outer', 'inner'))
Inputs may be any that keep to these rules, and one draw needn't show every extreme that they name: `doc_lengths`: the lengths add up to 65536; the longest is exactly 1024.
All inputs are finite; a program needn't handle non-finite values.
Results may differ from a plain program's by a relative error of at most 0.0045.
Values may be sent and summed in bfloat16 or wider, within the bound.
No kernel may reach another device: no remote copies, remote signals or barrier semaphores. Data moves between devices by JAX's collectives and lax.ppermute only.
A program may use at most 64 MiB of HBM per device.

v0:
```python
import math

import jax
import jax.numpy as jnp
from jax import lax
from jax.sharding import PartitionSpec as P

SPAN = 2


NEG_FILL = -1e30


def shifted(value, axis, steps):
    count = lax.axis_size(axis)
    first, last = (max(0, -steps), min(count, count - steps))
    return lax.ppermute(value, axis, [(source, source + steps) for source in range(first, last)])


def document_of(positions, doc_lengths):
    boundary = jnp.cumsum(doc_lengths)
    return jnp.sum((boundary[None, :] <= positions[:, None]).astype(jnp.int32), axis=1)


def empty_status(row_count, head_count, head_width):
    return (
        jnp.full((row_count, head_count), NEG_FILL, jnp.float32),
        jnp.zeros((row_count, head_count), jnp.float32),
        jnp.zeros((row_count, head_count, head_width), jnp.float32),
    )


def attend_block(status, query_parts, key_slab, value_slab, key_pos, key_doc, slopes):
    query_rows, query_pos, query_doc = query_parts
    allowed = (query_doc[:, None] == key_doc[None, :]) & (key_pos[None, :] <= query_pos[:, None])

    def update(current):
        running_max, row_total, weighted_sum = current
        scores = jnp.einsum(
            "qhd,khd->qhk", query_rows, key_slab, preferred_element_type=jnp.float32
        )
        scores = scores * (1.0 / math.sqrt(query_rows.shape[-1]))
        distance = (query_pos[:, None] - key_pos[None, :]).astype(jnp.float32)
        scores = scores - slopes[None, :, None] * distance[:, None, :]
        scores = jnp.where(allowed[:, None, :], scores, NEG_FILL)
        new_max = jnp.maximum(running_max, jnp.max(scores, axis=-1))
        weights = jnp.where(allowed[:, None, :], jnp.exp(scores - new_max[:, :, None]), 0.0)
        rescale = jnp.exp(running_max - new_max)
        row_total = row_total * rescale + jnp.sum(weights, axis=-1)
        products = jnp.einsum(
            "qhk,khd->qhd",
            weights.astype(jnp.bfloat16),
            value_slab,
            preferred_element_type=jnp.float32,
        )
        weighted_sum = weighted_sum * rescale[:, :, None] + products
        return (new_max, row_total, weighted_sum)

    def unchanged(current):
        return current

    return lax.cond(jnp.any(allowed), update, unchanged, status)


def attend_keys(status, query_parts, key_slab, value_slab, key_pos, slopes, doc_lengths):
    key_doc = document_of(key_pos, doc_lengths)
    key_count = key_slab.shape[0]
    slab_rows = 256
    pieces = key_count // slab_rows
    stacked = (
        key_slab.reshape((pieces, slab_rows) + key_slab.shape[1:]),
        value_slab.reshape((pieces, slab_rows) + value_slab.shape[1:]),
        key_pos.reshape(pieces, slab_rows),
        key_doc.reshape(pieces, slab_rows),
    )

    def scan_step(current, portion):
        return (
            attend_block(
                current, query_parts, portion[0], portion[1], portion[2], portion[3], slopes
            ),
            None,
        )

    result, unused = lax.scan(scan_step, status, stacked)
    return result


def combine(first_status, second_status):
    new_max = jnp.maximum(first_status[0], second_status[0])
    left_scale = jnp.exp(first_status[0] - new_max)
    right_scale = jnp.exp(second_status[0] - new_max)
    return (
        new_max,
        first_status[1] * left_scale + second_status[1] * right_scale,
        first_status[2] * left_scale[:, :, None] + second_status[2] * right_scale[:, :, None],
    )


def queries_from_later(query_rows, hops_back):
    return shifted(query_rows, "outer", -hops_back)


def partials_home(status, hops_back):
    running_max, row_total, weighted_sum = status
    moved_max, moved_total, moved_sum = shifted(
        (running_max, row_total, weighted_sum), "outer", hops_back
    )
    return (jnp.where(moved_total > 0.0, moved_max, NEG_FILL), moved_total, moved_sum)


def rows_of(status, slot_index, row_count):
    return tuple(
        (member[slot_index * row_count : (slot_index + 1) * row_count] for member in status)
    )


def bring_home(status, row_count, span_count):
    own_status = rows_of(status, 0, row_count)
    distant = [rows_of(status, hops_back, row_count) for hops_back in range(1, span_count + 1)]
    merged = own_status
    for hops_back in range(1, span_count + 1):
        merged = combine(merged, partials_home(distant[hops_back - 1], hops_back))
    return merged


def with_later_queries(own_rows, own_pos, group_rows, span_count, doc_lengths):
    rows_list = [own_rows]
    pos_list = [own_pos]
    for hops_back in range(1, span_count + 1):
        rows_list.append(queries_from_later(own_rows, hops_back))
        pos_list.append(own_pos + hops_back * group_rows)
    all_pos = jnp.concatenate(pos_list)
    return (jnp.concatenate(rows_list, axis=0), all_pos, document_of(all_pos, doc_lengths))


def normalize(status):
    return (status[2] / status[1][:, :, None]).astype(jnp.bfloat16)


def per_device(query_states, key_states, value_states, doc_lengths, slopes):
    rows_dev = query_states.shape[0]
    head_count = slopes.shape[0]
    head_width = query_states.shape[1] // head_count
    inner_count = lax.axis_size("inner")
    group_index = lax.axis_index("outer")
    inner_index = lax.axis_index("inner")
    group_rows = rows_dev * inner_count
    group_start = group_index * group_rows
    own_queries = query_states.reshape(rows_dev, head_count, head_width)
    own_pos = group_start + inner_index * rows_dev + jnp.arange(rows_dev, dtype=jnp.int32)
    query_parts = with_later_queries(own_queries, own_pos, group_rows, SPAN, doc_lengths)
    status = empty_status(query_parts[0].shape[0], head_count, head_width)
    portions = (
        lax.all_gather(
            key_states.reshape(rows_dev, head_count, head_width), "inner", axis=0, tiled=True
        ),
        lax.all_gather(
            value_states.reshape(rows_dev, head_count, head_width), "inner", axis=0, tiled=True
        ),
    )
    key_pos = group_start + jnp.arange(portions[0].shape[0], dtype=jnp.int32)
    status = attend_keys(
        status, query_parts, portions[0], portions[1], key_pos, slopes, doc_lengths
    )
    combined = bring_home(status, rows_dev, SPAN)
    return normalize(combined).reshape(rows_dev, head_count * head_width)


def solution(mesh):
    placed = (
        P(("outer", "inner"), None),
        P(("outer", "inner"), None),
        P(("outer", "inner"), None),
        P(),
        P(),
    )
    return jax.shard_map(
        per_device,
        mesh=mesh,
        in_specs=placed,
        out_specs=P(("outer", "inner"), None),
        check_vma=False,
    )
```

profile of v0, /device:TPU:256, one launch (start us, length us, event | category | flops | bytes accessed | tf_op | source)
XLA Modules:
  0.0 273.0 jit_solution(12478321590578903642)
XLA Ops:
  6.5 2.5 copy.32
  9.1 2.4 copy.33
  12.3 3.9 %collective-permute-start = (bf16[128,32,128]{0,2,1:T(8,128)(2,1)S(1)}, bf16[128,32,128]{0,2,1:T(8,128)(2,1)S(1)}, u32[]{:S(2)}, u32[]{:S(2)}) collective-permute-start(bf16[128,32,128]{0,2,1:T(8,128)(2,1)S(1)} %bitcast.49), channel_id=1, source_target_pairs={{4,0},{8,4},{12,8},{16,12},{20,16},{24,20},{28,24},{32,28},{36,32}... | collective-permute-start | bytes 3145736 | tf_op jit(solution)/shard_map/ppermute | solution.py:17
  16.2 3.3 %collective-permute-start.1 = (bf16[128,32,128]{0,2,1:T(8,128)(2,1)S(1)}, bf16[128,32,128]{0,2,1:T(8,128)(2,1)}, u32[]{:S(2)}, u32[]{:S(2)}) collective-permute-start(bf16[128,32,128]{0,2,1:T(8,128)(2,1)S(1)} %bitcast.50), channel_id=1, source_target_pairs={{8,0},{12,4},{16,8},{20,12},{24,16},{28,20},{32,24},{36,28},{40,32... | collective-permute-start | bytes 3145736 | tf_op jit(solution)/shard_map/ppermute | solution.py:17
  20.4 17.2 %collective-permute-done = bf16[128,32,128]{0,2,1:T(8,128)(2,1)S(1)} collective-permute-done((bf16[128,32,128]{0,2,1:T(8,128)(2,1)S(1)}, bf16[128,32,128]{0,2,1:T(8,128)(2,1)S(1)}, u32[]{:S(2)}, u32[]{:S(2)}) %collective-permute-start) | collective-permute-done | bytes 1048608 | tf_op jit(solution)/shard_map/ppermute | solution.py:17
  38.7 12.4 %collective-permute-done.1 = bf16[128,32,128]{0,2,1:T(8,128)(2,1)} collective-permute-done((bf16[128,32,128]{0,2,1:T(8,128)(2,1)S(1)}, bf16[128,32,128]{0,2,1:T(8,128)(2,1)}, u32[]{:S(2)}, u32[]{:S(2)}) %collective-permute-start.1) | collective-permute-done | bytes 1048608 | tf_op jit(solution)/shard_map/ppermute | solution.py:17
  51.1 2.4 pad_maximum_fusion
  53.5 2.9 %copy.27 = bf16[384,32,128]{2,0,1:T(8,128)(2,1)} copy(bf16[384,32,128]{0,2,1:T(8,128)(2,1)S(1)} %pad_maximum_fusion) | data formatting | bytes 6291456 | tf_op jit(solution)/shard_map/while | solution.py:85
  56.4 8.4 %all-gather.3.cloned.1.call-done = bf16[512,32,128]{2,1,0:T(8,128)(2,1)} async-done(((bf16[128,32,128]{2,1,0:T(8,128)(2,1)}), bf16[512,32,128]{2,1,0:T(8,128)(2,1)}) %all-gather.3.cloned.1.call-update) | async-done | bytes 4194320 | tf_op jit(solution)/shard_map/all_gather | solution.py:155
  64.8 5.8 %copy.26 = bf16[2,256,32,128]{3,1,2,0:T(8,128)(2,1)} copy(bf16[2,256,32,128]{3,2,1,0:T(8,128)(2,1)} %bitcast.45) | data formatting | bytes 8388608 | tf_op jit(solution)/shard_map/while | solution.py:85
  70.7 50.3 %all-gather.5.cloned.1.call-done = bf16[512,32,128]{2,1,0:T(8,128)(2,1)} async-done(((bf16[128,32,128]{2,1,0:T(8,128)(2,1)}), bf16[512,32,128]{2,1,0:T(8,128)(2,1)}) %all-gather.5.cloned.1.call-update) | async-done | bytes 4194320 | tf_op jit(solution)/shard_map/all_gather | solution.py:158
  121.0 6.0 %copy.28 = bf16[2,256,32,128]{3,1,2,0:T(8,128)(2,1)} copy(bf16[2,256,32,128]{3,2,1,0:T(8,128)(2,1)} %bitcast.46) | data formatting | bytes 8388608 | tf_op jit(solution)/shard_map/while | solution.py:85
  127.0 3.4 %broadcast_in_dim.61 = f32[384,32,128]{2,0,1:T(8,128)} broadcast(f32[]{:T(128)} %constant.59.clone.1), dimensions={} | broadcast | bytes 6291460 | tf_op jit(solution)/shard_map/broadcast_in_dim | solution.py:29
  130.4 41.3 %while.14 = (s32[]{:T(128)}, f32[384,32]{0,1:T(8,128)S(1)}, f32[384,32]{0,1:T(8,128)S(1)}, f32[384,32,128]{2,0,1:T(8,128)}, s32[384]{0:T(512)S(1)}, /*index=5*/s...) while((s32[]{:T(128)}, f32[384,32]{0,1:T(8,128)S(1)}, ...), condition=%wide.region_9.10_spmd, body=%wide.region_3.9_spmd.sunk | while | flops 1674141696 | bytes 104477920 | solution.py:85
  131.9 19.2 %conditional.2 = ((f32[384,32]{0,1:T(8,128)S(1)}, f32[384,32]{0,1:T(8,128)S(1)}, f32[384,32,128]{2,0,1:T(8,128)})) conditional(s32[]{:T(128)} %convert_element_type.41, (f32[384,32]{0,1:T(8,128)S(1)}, f32[384,32]{0,1:T(8,128)S(1)}, f32[384,32,128]{2,0,1:T(8,128)}) %tuple.50, (pred[384,256]{0,1:T(8,128)(4,1)S(1)}, bf16[2,256,32,128]{3,1,2,0:T(8,128)(2,1)}, ...), branch_computations={%region_5.5_spmd, %region_6.8_spmd} | conditional | flops 1673748480 | bytes 104370152 | solution.py:62
  132.0 4.5 %fusion.3 = (f32[384,32]{0,1:T(8,128)S(1)}, f32[32,256,384]{2,1,0:T(8,128)S(1)}) fusion(f32[384,256]{0,1:T(8,128)S(1)} %subtract_convert_fusion, f32[32]{0:T(128)S(1)} %get-tuple-element.141, pred[384,256]{0,1:T(8,128)(4,1)S(1)} %get-tuple-element.137, bf16[384,32,128]{2,0,1:T(8,128)(2,1)S(1)} %get-tuple-element.140, ...), kind=kOutput, calls=%fused_computation.5 | convolution fusion | flops 821022720 | bytes 18367104 | tf_op jit(solution)/shard_map/while/body/eval_jaxpr/cond/branch_1_fun/qhd,khd->qhk/dot_general | solution.py:39
  136.6 4.3 %fusion.2 = f32[384,32]{0,1:T(8,128)S(1)} fusion(f32[32,256,384]{2,1,0:T(8,128)S(1)} %get-tuple-element.239, f32[384,32]{0,1:T(8,128)S(1)} %max.8, f32[384,256]{0,1:T(8,128)S(1)} %subtract_convert_fusion, f32[32]{0:T(128)S(1)} %get-tuple-element.141, pred[384,256]{0,1:T(8,128)(4,1)S(1)} %get-tuple-element.137), kind=kLoop, calls=%fused_computation.4 | loop fusion | flops 22007808 | bytes 13172864 | tf_op jit(solution)/shard_map/while/body/eval_jaxpr/cond/branch_1_fun/reduce_sum | solution.py:49
  140.9 7.5 %bitcast_add_fusion = f32[384,32,128]{2,0,1:T(8,128)S(1)} fusion(f32[384,32,128]{2,0,1:T(8,128)S(1)} %bitcast.44, f32[384,32]{0,1:T(8,128)S(1)} %get-tuple-element.230, f32[32,256,384]{2,1,0:T(8,128)S(1)} %get-tuple-element.239, f32[384,32]{0,1:T(8,128)S(1)} %max.8, f32[384,256]{0,1:T(8,128)S(1)} %subtract_convert_fusion, f32[32]{0:T(128)S(1)} %get-tuple-element.141, ...), kind=kOutput, calls=%fused_computation.6 | convolution fusion | flops 830472192 | bytes 27853440 | tf_op jit(solution)/shard_map/while/body/eval_jaxpr/cond/branch_1_fun/qhk,khd->qhd/dot_general | solution.py:50
  148.4 2.7 copy-done
  152.5 19.2 %conditional.2 = ((f32[384,32]{0,1:T(8,128)S(1)}, f32[384,32]{0,1:T(8,128)S(1)}, f32[384,32,128]{2,0,1:T(8,128)})) conditional(s32[]{:T(128)} %convert_element_type.41, (f32[384,32]{0,1:T(8,128)S(1)}, f32[384,32]{0,1:T(8,128)S(1)}, f32[384,32,128]{2,0,1:T(8,128)}) %tuple.50, (pred[384,256]{0,1:T(8,128)(4,1)S(1)}, bf16[2,256,32,128]{3,1,2,0:T(8,128)(2,1)}, ...), branch_computations={%region_5.5_spmd, %region_6.8_spmd} | conditional | flops 1673748480 | bytes 104370152 | solution.py:62
  152.7 4.5 %fusion.3 = (f32[384,32]{0,1:T(8,128)S(1)}, f32[32,256,384]{2,1,0:T(8,128)S(1)}) fusion(f32[384,256]{0,1:T(8,128)S(1)} %subtract_convert_fusion, f32[32]{0:T(128)S(1)} %get-tuple-element.141, pred[384,256]{0,1:T(8,128)(4,1)S(1)} %get-tuple-element.137, bf16[384,32,128]{2,0,1:T(8,128)(2,1)S(1)} %get-tuple-element.140, ...), kind=kOutput, calls=%fused_computation.5 | convolution fusion | flops 821022720 | bytes 18367104 | tf_op jit(solution)/shard_map/while/body/eval_jaxpr/cond/branch_1_fun/qhd,khd->qhk/dot_general | solution.py:39
  157.2 4.3 %fusion.2 = f32[384,32]{0,1:T(8,128)S(1)} fusion(f32[32,256,384]{2,1,0:T(8,128)S(1)} %get-tuple-element.239, f32[384,32]{0,1:T(8,128)S(1)} %max.8, f32[384,256]{0,1:T(8,128)S(1)} %subtract_convert_fusion, f32[32]{0:T(128)S(1)} %get-tuple-element.141, pred[384,256]{0,1:T(8,128)(4,1)S(1)} %get-tuple-element.137), kind=kLoop, calls=%fused_computation.4 | loop fusion | flops 22007808 | bytes 13172864 | tf_op jit(solution)/shard_map/while/body/eval_jaxpr/cond/branch_1_fun/reduce_sum | solution.py:49
  161.6 7.5 %bitcast_add_fusion = f32[384,32,128]{2,0,1:T(8,128)S(1)} fusion(f32[384,32,128]{2,0,1:T(8,128)S(1)} %bitcast.44, f32[384,32]{0,1:T(8,128)S(1)} %get-tuple-element.230, f32[32,256,384]{2,1,0:T(8,128)S(1)} %get-tuple-element.239, f32[384,32]{0,1:T(8,128)S(1)} %max.8, f32[384,256]{0,1:T(8,128)S(1)} %subtract_convert_fusion, f32[32]{0:T(128)S(1)} %get-tuple-element.141, ...), kind=kOutput, calls=%fused_computation.6 | convolution fusion | flops 830472192 | bytes 27853440 | tf_op jit(solution)/shard_map/while/body/eval_jaxpr/cond/branch_1_fun/qhk,khd->qhd/dot_general | solution.py:50
  169.1 2.7 copy-done
  171.7 2.5 fusion.25
  176.1 3.4 %collective-permute-start.7 = (f32[128,32,128]{2,0,1:T(8,128)S(1)}, f32[128,32,128]{2,0,1:T(8,128)S(1)}, u32[]{:S(2)}, u32[]{:S(2)}) collective-permute-start(f32[128,32,128]{2,0,1:T(8,128)S(1)} %get-tuple-element.243), channel_id=1, source_target_pairs={{0,8},{4,12},{8,16},{12,20},{16,24},{20,28},{24,32},{28,36},{32,40... | collective-permute-start | bytes 6291464 | tf_op jit(solution)/shard_map/ppermute | solution.py:17
  179.6 3.2 %collective-permute-start.2 = (f32[128,32]{0,1:T(8,128)S(1)}, f32[128,32]{0,1:T(8,128)S(1)}, u32[]{:S(2)}, u32[]{:S(2)}) collective-permute-start(f32[128,32]{0,1:T(8,128)S(1)} %get-tuple-element.246), channel_id=1, source_target_pairs={{0,4},{4,8},{8,12},{12,16},{16,20},{20,24},{24,28},{28,32},{32,36}... | collective-permute-start | bytes 49160 | tf_op jit(solution)/shard_map/ppermute | solution.py:17
  182.8 2.2 collective-permute-start.3
  185.0 3.4 %collective-permute-start.5 = (f32[128,32]{0,1:T(8,128)S(1)}, f32[128,32]{0,1:T(8,128)S(1)}, u32[]{:S(2)}, u32[]{:S(2)}) collective-permute-start(f32[128,32]{0,1:T(8,128)S(1)} %get-tuple-element.247), channel_id=1, source_target_pairs={{0,8},{4,12},{8,16},{12,20},{16,24},{20,28},{24,32},{28,36},{32,40... | collective-permute-start | bytes 49160 | tf_op jit(solution)/shard_map/ppermute | solution.py:17
  188.4 61.8 %collective-permute-done.2 = f32[128,32]{0,1:T(8,128)S(1)} collective-permute-done((f32[128,32]{0,1:T(8,128)S(1)}, f32[128,32]{0,1:T(8,128)S(1)}, u32[]{:S(2)}, u32[]{:S(2)}) %collective-permute-start.2) | collective-permute-done | bytes 16416 | tf_op jit(solution)/shard_map/ppermute | solution.py:17
  252.1 7.0 %collective-permute-done.6 = f32[128,32]{0,1:T(8,128)S(1)} collective-permute-done((f32[128,32]{0,1:T(8,128)S(1)}, f32[128,32]{0,1:T(8,128)S(1)}, u32[]{:S(2)}, u32[]{:S(2)}) %collective-permute-start.6) | collective-permute-done | bytes 16416 | tf_op jit(solution)/shard_map/ppermute | solution.py:17
  259.2 7.0 %copy_bitcast_fusion = bf16[128,4096]{1,0:T(8,128)(2,1)} fusion(f32[128,32]{0,1:T(8,128)S(1)} %get-tuple-element.233, f32[128,32,128]{2,0,1:T(8,128)S(1)} %collective-permute-done.7, f32[128,32]{0,1:T(8,128)S(1)} %get-tuple-element.237, f32[128,32]{0,1:T(8,128)S(1)} %get-tuple-element.236, f32[128,32,128]{2,0,1:T(8,128)S(1)} %collective-permute-done.4, ...), kind=kLoop, calls=%fused_computation.27 | loop fusion | flops 4194304 | bytes 7421952 | tf_op jit(solution)/shard_map/reshape | solution.py:167
  (63 shorter events, 8.5 us)
Async XLA Ops:
  6.5 5.1 %copy-start.3 = (bf16[128,4096]{1,0:T(8,128)(2,1)S(1)}, bf16[128,4096]{1,0:T(8,128)(2,1)}, u32[]{:S(2)}) copy-start(bf16[128,4096]{1,0:T(8,128)(2,1)} %param.9) | copy-start | bytes 3145732
  6.5 12.9 %copy-start.6 = (s32[128]{0:T(128)S(1)}, s32[128]{0:T(128)}, u32[]{:S(2)}) copy-start(s32[128]{0:T(128)} %param.12) | copy-start | bytes 1540
  6.5 58.3 %all-gather.3.cloned.1.call-start = ((), (), s32[]{:S(2)}) async-start(), calls=%async_computation | async-start | bytes 5242880 | tf_op jit(solution)/shard_map/all_gather | solution.py:155
  9.1 111.9 %all-gather.5.cloned.1.call-start = ((), (), s32[]{:S(2)}) async-start(), calls=%async_computation.1 | async-start | bytes 5242880 | tf_op jit(solution)/shard_map/all_gather | solution.py:158
  12.3 25.4 %copy-start.1 = (bf16[128,4096]{0,1:T(8,128)(2,1)}, bf16[128,4096]{0,1:T(8,128)(2,1)S(1)}, u32[]{:S(2)}) copy-start(bf16[128,4096]{0,1:T(8,128)(2,1)S(1)} %copy.25) | copy-start | bytes 3145732
  12.3 25.4 %collective-permute-start = (bf16[128,32,128]{0,2,1:T(8,128)(2,1)S(1)}, bf16[128,32,128]{0,2,1:T(8,128)(2,1)S(1)}, u32[]{:S(2)}, u32[]{:S(2)}) collective-permute-start(bf16[128,32,128]{0,2,1:T(8,128)(2,1)S(1)} %bitcast.49), channel_id=1, source_target_pairs={{4,0},{8,4},{12,8},{16,12},{20,16},{24,20},{28,24},{32,28},{36,32}... | collective-permute-start | bytes 3145736 | tf_op jit(solution)/shard_map/ppermute | solution.py:17
  16.2 34.9 %collective-permute-start.1 = (bf16[128,32,128]{0,2,1:T(8,128)(2,1)S(1)}, bf16[128,32,128]{0,2,1:T(8,128)(2,1)}, u32[]{:S(2)}, u32[]{:S(2)}) collective-permute-start(bf16[128,32,128]{0,2,1:T(8,128)(2,1)S(1)} %bitcast.50), channel_id=1, source_target_pairs={{8,0},{12,4},{16,8},{20,12},{24,16},{28,20},{32,24},{36,28},{40,32... | collective-permute-start | bytes 3145736 | tf_op jit(solution)/shard_map/ppermute | solution.py:17
  37.6 1.0 copy-start.4
  121.0 9.4 %copy-start.2 = (bf16[384,32,128]{2,0,1:T(8,128)(2,1)S(1)}, bf16[384,32,128]{2,0,1:T(8,128)(2,1)}, u32[]{:S(2)}) copy-start(bf16[384,32,128]{2,0,1:T(8,128)(2,1)} %copy.27) | copy-start | bytes 9437188
  121.0 9.4 %copy-start.5 = (f32[32]{0:T(128)S(1)}, f32[32]{0:T(128)}, u32[]{:S(2)}) copy-start(f32[32]{0:T(128)} %param.13) | copy-start | bytes 388
  131.9 9.0 %slice-start = ((s8[6291456]{0:T(1024)(128)(4,1)}), s8[4194304]{0:T(1024)(128)(4,1)S(1)}, s32[]{:S(2)}) async-start(s8[6291456]{0:T(1024)(128)(4,1)} %bitcast.43), calls=%async_computation.2 | async-start | bytes 8388608 | tf_op jit(solution)/shard_map/while/body/eval_jaxpr/cond
  132.0 8.9 %slice-start.1 = ((s8[6291456]{0:T(1024)(128)(4,1)}), s8[2097152]{0:T(1024)(128)(4,1)S(1)}, s32[]{:S(2)}) async-start(s8[6291456]{0:T(1024)(128)(4,1)} %bitcast.43), calls=%async_computation.3 | async-start | bytes 4194304 | tf_op jit(solution)/shard_map/while/body/eval_jaxpr/cond
  148.4 2.7 copy-start
  152.5 9.0 %slice-start = ((s8[6291456]{0:T(1024)(128)(4,1)}), s8[4194304]{0:T(1024)(128)(4,1)S(1)}, s32[]{:S(2)}) async-start(s8[6291456]{0:T(1024)(128)(4,1)} %bitcast.43), calls=%async_computation.2 | async-start | bytes 8388608 | tf_op jit(solution)/shard_map/while/body/eval_jaxpr/cond
  152.7 8.9 %slice-start.1 = ((s8[6291456]{0:T(1024)(128)(4,1)}), s8[2097152]{0:T(1024)(128)(4,1)S(1)}, s32[]{:S(2)}) async-start(s8[6291456]{0:T(1024)(128)(4,1)} %bitcast.43), calls=%async_computation.3 | async-start | bytes 4194304 | tf_op jit(solution)/shard_map/while/body/eval_jaxpr/cond
  169.0 2.7 copy-start
  174.2 84.9 %collective-permute-start.4 = (f32[128,32,128]{2,0,1:T(8,128)S(1)}, f32[128,32,128]{2,0,1:T(8,128)S(1)}, u32[]{:S(2)}, u32[]{:S(2)}) collective-permute-start(f32[128,32,128]{2,0,1:T(8,128)S(1)} %get-tuple-element.242), channel_id=1, source_target_pairs={{0,4},{4,8},{8,12},{12,16},{16,20},{20,24},{24,28},{28,32},{32,36}... | collective-permute-start | bytes 6291464 | tf_op jit(solution)/shard_map/ppermute | solution.py:17
  176.1 83.0 %collective-permute-start.7 = (f32[128,32,128]{2,0,1:T(8,128)S(1)}, f32[128,32,128]{2,0,1:T(8,128)S(1)}, u32[]{:S(2)}, u32[]{:S(2)}) collective-permute-start(f32[128,32,128]{2,0,1:T(8,128)S(1)} %get-tuple-element.243), channel_id=1, source_target_pairs={{0,8},{4,12},{8,16},{12,20},{16,24},{20,28},{24,32},{28,36},{32,40... | collective-permute-start | bytes 6291464 | tf_op jit(solution)/shard_map/ppermute | solution.py:17
  179.6 70.6 %collective-permute-start.2 = (f32[128,32]{0,1:T(8,128)S(1)}, f32[128,32]{0,1:T(8,128)S(1)}, u32[]{:S(2)}, u32[]{:S(2)}) collective-permute-start(f32[128,32]{0,1:T(8,128)S(1)} %get-tuple-element.246), channel_id=1, source_target_pairs={{0,4},{4,8},{8,12},{12,16},{16,20},{20,24},{24,28},{28,32},{32,36}... | collective-permute-start | bytes 49160 | tf_op jit(solution)/shard_map/ppermute | solution.py:17
  182.8 69.3 %collective-permute-start.3 = (f32[128,32]{0,1:T(8,128)S(1)}, f32[128,32]{0,1:T(8,128)S(1)}, u32[]{:S(2)}, u32[]{:S(2)}) collective-permute-start(f32[128,32]{0,1:T(8,128)S(1)} %get-tuple-element.245), channel_id=1, source_target_pairs={{0,4},{4,8},{8,12},{12,16},{16,20},{20,24},{24,28},{28,32},{32,36}... | collective-permute-start | bytes 49160 | tf_op jit(solution)/shard_map/ppermute | solution.py:17
  185.0 67.1 %collective-permute-start.5 = (f32[128,32]{0,1:T(8,128)S(1)}, f32[128,32]{0,1:T(8,128)S(1)}, u32[]{:S(2)}, u32[]{:S(2)}) collective-permute-start(f32[128,32]{0,1:T(8,128)S(1)} %get-tuple-element.247), channel_id=1, source_target_pairs={{0,8},{4,12},{8,16},{12,20},{16,24},{20,28},{24,32},{28,36},{32,40... | collective-permute-start | bytes 49160 | tf_op jit(solution)/shard_map/ppermute | solution.py:17
  250.2 8.9 %collective-permute-start.6 = (f32[128,32]{0,1:T(8,128)S(1)}, f32[128,32]{0,1:T(8,128)S(1)}, u32[]{:S(2)}, u32[]{:S(2)}) collective-permute-start(f32[128,32]{0,1:T(8,128)S(1)} %get-tuple-element.244), channel_id=1, source_target_pairs={{0,8},{4,12},{8,16},{12,20},{16,24},{20,28},{24,32},{28,36},{32,40... | collective-permute-start | bytes 49160 | tf_op jit(solution)/shard_map/ppermute | solution.py:17
Sparse Core Ops, SparseCore 0:
  9.5 55.3 all-gather.2
  66.9 53.9 all-gather.4
where the time goes:
time: 274 us; the launch traced here: 273 us
  waiting for transfers between devices  157 us (57%)
  local copies, waits for them, and re-layouts  32.9 us (12%)
  matrix products  24 us (9%)
  starting transfers between devices  23.2 us (8%)
  other arithmetic  20.6 us (8%)
  between operations  13.6 us (5%)
    ppermute x8, waiting for transfers between devices, shifted(): lax.ppermute(value, axis, [(source, source + steps) for source in range(f...  98.4 us
    all_gather x1, waiting for transfers between devices, per_device(): lax.all_gather(value_states.reshape(rows_dev, head_count, head_width), 'i...  50.3 us
    ppermute x8, starting transfers between devices, shifted(): lax.ppermute(value, axis, [(source, source + steps) for source in range(f...  23.2 us
    dot_general x2, matrix products, update(): jnp.einsum('qhk,khd->qhd', weights.astype(jnp.bfloat16), value_slab, pref...  15 us
    while x3, local copies, waits for them, and re-layouts, attend_keys(): result, unused = lax.scan(scan_step, status, stacked)  14.8 us
    dot_general x2, matrix products, update(): jnp.einsum('qhd,khd->qhk', query_rows, key_slab, preferred_element_type=j...  9.01 us
    reduce_sum x2, other arithmetic, update(): row_total = row_total * rescale + jnp.sum(weights, axis=-1)  8.57 us
    all_gather x1, waiting for transfers between devices, per_device(): lax.all_gather(key_states.reshape(rows_dev, head_count, head_width), 'inn...  8.4 us
  transfers between devices with their start and end apart: 10, of which 6 were waited for; matrix products, arithmetic and copies ran while one was open for 6% of the time, Pallas kernels for 0%

commit v1 on v0

v1 whole, which is shorter than its diff:
```python
import functools
import math

import jax
import jax.numpy as jnp
from jax import lax
from jax.experimental import pallas as pl
from jax.experimental.pallas import tpu as pltpu
from jax.sharding import PartitionSpec as P

AXES = ("outer", "inner")
TILE = 256
NEG_FILL = -1e30
LOG2E = math.log2(math.e)


def pack_kernel(heads, count, *refs):
    sources, out_ref = refs[:-1], refs[-1]
    groups = out_ref.shape[0]
    for group in range(groups):
        place = 0
        for source in sources:
            for head in heads:
                column = (group * count + head) * 128
                out_ref[group, :, place : place + 128] = source[:, column : column + 128]
                place += 128


def pack(sources, heads, count, groups):
    rows = sources[0].shape[0]
    width = len(sources) * len(heads) * 128
    return pl.pallas_call(
        functools.partial(pack_kernel, heads, count),
        out_shape=jax.ShapeDtypeStruct((groups, rows, width), jnp.bfloat16),
        in_specs=[pl.BlockSpec(memory_space=pltpu.VMEM)] * len(sources),
        out_specs=pl.BlockSpec(memory_space=pltpu.VMEM),
        compiler_params=pltpu.CompilerParams(vmem_limit_bytes=16 << 20),
        cost_estimate=pl.CostEstimate(
            flops=0, bytes_accessed=4 * groups * rows * width, transcendentals=0
        ),
    )(*sources)


def unpack_kernel(recv_ref, out_ref):
    groups, _, width = recv_ref.shape
    for group in range(groups):
        out_ref[:, group * width : (group + 1) * width] = recv_ref[group]


def unpack(recv):
    groups, rows, width = recv.shape
    return pl.pallas_call(
        unpack_kernel,
        out_shape=jax.ShapeDtypeStruct((rows, groups * width), jnp.bfloat16),
        in_specs=[pl.BlockSpec(memory_space=pltpu.VMEM)],
        out_specs=pl.BlockSpec(memory_space=pltpu.VMEM),
        compiler_params=pltpu.CompilerParams(vmem_limit_bytes=16 << 20),
    )(recv)


def attend_kernel(
    inv_root, first, tiles_ref, slopes_ref, start_ref, q_ref, kl_ref, vl_ref, kh_ref, vh_ref,
    out_ref, key_win, value_win,
):
    span = q_ref.shape[0]
    tiles = span // TILE
    most = span // TILE + 1

    @pl.when(pl.program_id(0) == 0)
    def _():
        value_win[:, 128:] = jnp.ones((2 * span, 128), jnp.bfloat16)

    key_win[:span, :] = kh_ref[...]
    key_win[span:, :] = kl_ref[...]
    value_win[:span, :128] = vh_ref[...]
    value_win[span:, :128] = vl_ref[...]
    slope = slopes_ref[first + pl.program_id(0)] * LOG2E

    def one_tile(tile, _):
        row = pl.multiple_of(tile * TILE, TILE)
        needed = tiles_ref[tile]

        for count in range(1, most + 1):

            @pl.when(needed == count)
            def _():
                width = count * TILE
                base = pl.multiple_of((tile + tiles + 1 - count) * TILE, TILE)
                scores = lax.dot_general(
                    q_ref[pl.ds(row, TILE), :],
                    key_win[pl.ds(base, width), :],
                    (((1,), (1,)), ((), ())),
                    preferred_element_type=jnp.float32,
                )
                offset = lax.broadcasted_iota(jnp.int32, (1, width), 1)
                bias = slope * (offset - width).astype(jnp.float32)
                scores = scores * (inv_root * LOG2E) + bias
                begin = start_ref[pl.ds(row, TILE), :] - base
                scores = jnp.where(offset >= begin, scores, NEG_FILL)
                row_in = lax.broadcasted_iota(jnp.int32, (TILE, TILE), 0)
                column_in = lax.broadcasted_iota(jnp.int32, (TILE, TILE), 1)
                last = jnp.where(column_in <= row_in, scores[:, width - TILE :], NEG_FILL)
                if count > 1:
                    scores = jnp.concatenate([scores[:, : width - TILE], last], axis=1)
                else:
                    scores = last
                row_max = jnp.max(scores, axis=1, keepdims=True)
                weights = jnp.exp2(scores - row_max).astype(jnp.bfloat16)
                both = lax.dot_general(
                    weights,
                    value_win[pl.ds(base, width), :],
                    (((1,), (0,)), ((), ())),
                    preferred_element_type=jnp.float32,
                )
                out_ref[pl.ds(row, TILE), :] = (both[:, :128] / both[:, 128:]).astype(
                    jnp.bfloat16
                )

        return 0

    lax.fori_loop(0, tiles, one_tile, 0)


def attend(tiles_needed, slopes, starts, queries, own, halo, first, heads, q_first):
    span = queries.shape[0]

    def columns(offset):
        return pl.BlockSpec((span, 128), lambda i: (0, offset + i))

    smem = pl.BlockSpec(memory_space=pltpu.SMEM)
    return pl.pallas_call(
        functools.partial(attend_kernel, 1.0 / math.sqrt(128), first),
        grid=(heads,),
        out_shape=jax.ShapeDtypeStruct((span, heads * 128), jnp.bfloat16),
        in_specs=[
            smem,
            smem,
            pl.BlockSpec((span, 1), lambda i: (0, 0)),
            columns(q_first),
            columns(0),
            columns(heads),
            columns(0),
            columns(heads),
        ],
        out_specs=columns(0),
        scratch_shapes=[
            pltpu.VMEM((2 * span, 128), jnp.bfloat16),
            pltpu.VMEM((2 * span, 256), jnp.bfloat16),
        ],
        compiler_params=pltpu.CompilerParams(vmem_limit_bytes=40 << 20),
        cost_estimate=pl.CostEstimate(
            flops=heads * 4 * span * (span + TILE) * 128,
            bytes_accessed=heads * span * 128 * 12,
            transcendentals=heads * span * (span + TILE),
        ),
    )(tiles_needed, slopes, starts, queries, own, own, halo, halo)


def per_device(query_states, key_states, value_states, doc_lengths, slopes):
    rows = query_states.shape[0]
    outer, inner = lax.axis_size("outer"), lax.axis_size("inner")
    groups = 2 * inner
    supers = outer * inner // groups
    span = groups * rows
    count = slopes.shape[0] // groups
    me = lax.axis_index("outer") * inner + lax.axis_index("inner")
    super_index, member = me // groups, me % groups
    index_groups = [[s * groups + m for m in range(groups)] for s in range(supers)]
    onward = [(i, i + groups) for i in range((supers - 1) * groups)]

    def exchange(value):
        got = lax.all_to_all(value, AXES, 0, 0, axis_index_groups=index_groups)
        return got.reshape(span, value.shape[-1])

    half = count // 2
    parts = [tuple(range(half)), tuple(range(half, count))]
    own, halo = [], []
    for heads in parts:
        own.append(exchange(pack([key_states, value_states], heads, count, groups)))
        halo.append(lax.ppermute(own[-1], AXES, onward))
    queries = exchange(pack([query_states], tuple(range(count)), count, groups))

    ids = jnp.arange(doc_lengths.shape[0])
    ends = jnp.sum(jnp.where(ids[:, None] <= ids[None, :], doc_lengths[:, None], 0), axis=0)
    position = super_index * span + jnp.arange(span, dtype=jnp.int32)
    starts = jnp.max(jnp.where(ends[None, :] <= position[:, None], ends[None, :], 0), axis=1)
    starts = starts - (super_index - 1) * span
    tiles = span // TILE
    needed = jnp.arange(tiles) + tiles + 1 - starts[::TILE] // TILE
    my_slopes = lax.dynamic_slice(slopes, (member * count,), (count,))

    outs = []
    for i, heads in enumerate(parts):
        outs.append(
            attend(
                needed, my_slopes, starts[:, None], queries, own[i], halo[i],
                heads[0], len(heads), heads[0],
            )
        )
    out = jnp.concatenate(outs, axis=1).reshape(groups, rows, count * 128)
    back = lax.all_to_all(out, AXES, 0, 0, axis_index_groups=index_groups)
    return unpack(back)


def solution(mesh):
    tokens = P(AXES, None)
    return jax.shard_map(
        per_device,
        mesh=mesh,
        in_specs=(tokens, tokens, tokens, P(), P()),
        out_specs=tokens,
        check_vma=False,
    )
```

time: 274 us -> 110 us (0.40)
  waiting for transfers between devices: 157 us -> 45 us
  local copies, waits for them, and re-layouts: 32.9 us -> 7.63 us
  matrix products: 24 us -> 0 us
  other arithmetic: 20.6 us -> 0.56 us
  blocking collectives: 0 us -> 19.6 us
  Pallas kernels: 0 us -> 17.3 us
  between operations: 13.6 us -> 0.19 us
  starting transfers between devices: 23.2 us -> 18.6 us
    ppermute x8 -> x2, waiting for transfers between devices: 98.4 us -> 5.43 us  [per_device(): halo.append(lax.ppermute(own[-1], AXES, onward))]
    all_gather x2 -> x0, waiting for transfers between devices: 58.7 us -> none  [the longest x1 50.3 us: per_device(): lax.all_gather(value_states.reshape(rows_dev, head_count, head_width), 'i...]
    all_to_all x0 -> x3, waiting for transfers between devices: none -> 39.5 us  [exchange(): got = lax.all_to_all(value, AXES, 0, 0, axis_index_groups=index_groups)]
    dot_general x4 -> x0, matrix products: 24 us -> none  [the longest x2 15 us: update(): jnp.einsum('qhk,khd->qhd', weights.astype(jnp.bfloat16), value_slab, pref...]
    all_to_all x0 -> x1, blocking collectives: none -> 19.6 us  [per_device(): back = lax.all_to_all(out, AXES, 0, 0, axis_index_groups=index_groups)]
    pallas_call x0 -> x6, Pallas kernels: none -> 17.3 us  [the longest x2 16 us: attend(): pl.pallas_call(functools.partial(attend_kernel, 1.0 / math.sqrt(128), fir...]
    ppermute x8 -> x2, starting transfers between devices: 23.2 us -> 6.96 us  [per_device(): halo.append(lax.ppermute(own[-1], AXES, onward))]
    while x3 -> x0, local copies, waits for them, and re-layouts: 14.8 us -> none  [attend_keys(): result, unused = lax.scan(scan_step, status, stacked)]
  transfers between devices with their start and end apart: 10 -> 5, of which waited for: 6 -> 4; matrix products, arithmetic and copies ran while one was open for 6% -> 2% of each run, Pallas kernels for 0% -> 8%
where the time goes in v1:
time: 110 us; the launch traced here: 109 us
  waiting for transfers between devices  45 us (41%)
  blocking collectives  19.6 us (18%)
  starting transfers between devices  18.6 us (17%)
  Pallas kernels  17.3 us (16%)
  local copies, waits for them, and re-layouts  7.63 us (7%)
    all_to_all x3, waiting for transfers between devices, exchange(): got = lax.all_to_all(value, AXES, 0, 0, axis_index_groups=index_groups)  39.5 us
    all_to_all x1, blocking collectives, per_device(): back = lax.all_to_all(out, AXES, 0, 0, axis_index_groups=index_groups)  19.6 us
    pallas_call x2, Pallas kernels, attend(): pl.pallas_call(functools.partial(attend_kernel, 1.0 / math.sqrt(128), fir...  16 us
    all_to_all x3, starting transfers between devices, exchange(): got = lax.all_to_all(value, AXES, 0, 0, axis_index_groups=index_groups)  11.7 us
    ppermute x2, starting transfers between devices, per_device(): halo.append(lax.ppermute(own[-1], AXES, onward))  6.96 us
    unnamed x22, local copies, waits for them, and re-layouts  6.43 us
    ppermute x2, waiting for transfers between devices, per_device(): halo.append(lax.ppermute(own[-1], AXES, onward))  5.43 us
  transfers between devices with their start and end apart: 5, of which 4 were waited for; matrix products, arithmetic and copies ran while one was open for 2% of the time, Pallas kernels for 8%

profile of v1, /device:TPU:256, one launch (start us, length us, event | category | flops | bytes accessed | tf_op | source)
XLA Modules:
  0.0 108.9 jit_solution(12620931776079004463)
XLA Ops:
  0.0 1.2 %copy-done.1 = bf16[128,4096]{1,0:T(8,128)(2,1)S(1)} copy-done((bf16[128,4096]{1,0:T(8,128)(2,1)S(1)}, bf16[128,4096]{1,0:T(8,128)(2,1)}, u32[]{:S(2)}) %copy-start.1) | copy-done | bytes 1048600
  1.2 1.2 %copy-done.3 = bf16[128,4096]{1,0:T(8,128)(2,1)S(1)} copy-done((bf16[128,4096]{1,0:T(8,128)(2,1)S(1)}, bf16[128,4096]{1,0:T(8,128)(2,1)}, u32[]{:S(2)}) %copy-start.3) | copy-done | bytes 1048600
  2.5 0.1 shard_map.58
  2.5 0.0 copy-start.6
  2.5 1.0 copy-done.6
  3.5 4.4 %all-to-all-start.2 = ((bf16[8,128,512]{2,1,0:T(8,128)(2,1)}), bf16[8,128,512]{2,1,0:T(8,128)(2,1)S(1)}, u32[]{:S(2)}, u32[]{:S(2)}) async-start(bf16[8,128,512]{2,1,0:T(8,128)(2,1)} %copy-done.6), calls=%async_computation.2 | async-start | bytes 2097152 | tf_op jit(solution)/shard_map/all_to_all | solution.py:172
  8.0 0.1 shard_map.56
  8.0 0.0 copy-start.5
  8.1 1.0 copy-done.5
  9.1 14.2 %all-to-all-done.2 = bf16[8,128,512]{2,1,0:T(8,128)(2,1)S(1)} async-done(((bf16[8,128,512]{2,1,0:T(8,128)(2,1)}), bf16[8,128,512]{2,1,0:T(8,128)(2,1)S(1)}, u32[]{:S(2)}, u32[]{:S(2)}) %all-to-all-start.2) | async-done | bytes 1048608 | tf_op jit(solution)/shard_map/all_to_all | solution.py:172
  23.3 3.6 %all-to-all-start.1 = ((bf16[8,128,512]{2,1,0:T(8,128)(2,1)}), bf16[8,128,512]{2,1,0:T(8,128)(2,1)S(1)}, u32[]{:S(2)}, u32[]{:S(2)}) async-start(bf16[8,128,512]{2,1,0:T(8,128)(2,1)} %copy-done.5), calls=%async_computation.1 | async-start | bytes 2097152 | tf_op jit(solution)/shard_map/all_to_all | solution.py:172
  26.9 3.5 %collective-permute-start.1 = (bf16[1024,512]{1,0:T(8,128)(2,1)S(1)}, bf16[1024,512]{1,0:T(8,128)(2,1)}, u32[]{:S(2)}, u32[]{:S(2)}) collective-permute-start(bf16[1024,512]{1,0:T(8,128)(2,1)S(1)} %bitcast.5), channel_id=1, source_target_pairs={{0,8},{1,9},{2,10},{3,11},{4,12},{5,13},{6,14},{7,15},{8,16},{9,17... | collective-permute-start | bytes 3145736 | tf_op jit(solution)/shard_map/ppermute | solution.py:180
  30.3 11.8 %all-to-all-done.1 = bf16[8,128,512]{2,1,0:T(8,128)(2,1)S(1)} async-done(((bf16[8,128,512]{2,1,0:T(8,128)(2,1)}), bf16[8,128,512]{2,1,0:T(8,128)(2,1)S(1)}, u32[]{:S(2)}, u32[]{:S(2)}) %all-to-all-start.1) | async-done | bytes 1048608 | tf_op jit(solution)/shard_map/all_to_all | solution.py:172
  42.1 3.5 %collective-permute-start = (bf16[1024,512]{1,0:T(8,128)(2,1)S(1)}, bf16[1024,512]{1,0:T(8,128)(2,1)}, u32[]{:S(2)}, u32[]{:S(2)}) collective-permute-start(bf16[1024,512]{1,0:T(8,128)(2,1)S(1)} %bitcast.8), channel_id=1, source_target_pairs={{0,8},{1,9},{2,10},{3,11},{4,12},{5,13},{6,14},{7,15},{8,16},{9,17... | collective-permute-start | bytes 3145736 | tf_op jit(solution)/shard_map/ppermute | solution.py:180
  45.6 0.1 shard_map.55
  45.7 0.0 copy-start.7
  45.7 1.0 copy-done.7
  46.7 3.7 %all-to-all-start = ((bf16[8,128,512]{2,1,0:T(8,128)(2,1)}), bf16[8,128,512]{2,1,0:T(8,128)(2,1)S(1)}, u32[]{:S(2)}, u32[]{:S(2)}) async-start(bf16[8,128,512]{2,1,0:T(8,128)(2,1)} %copy-done.7), calls=%async_computation | async-start | bytes 2097152 | tf_op jit(solution)/shard_map/all_to_all | solution.py:172
  50.4 0.1 select_reduce_fusion.1
  50.5 0.4 select_reduce_fusion
  50.9 0.1 slice.3
  51.0 1.0 copy.8.start_ref
  52.0 0.1 dynamic_slice.3.slopes_ref
  52.1 13.5 %all-to-all-done = bf16[8,128,512]{2,1,0:T(8,128)(2,1)S(1)} async-done(((bf16[8,128,512]{2,1,0:T(8,128)(2,1)}), bf16[8,128,512]{2,1,0:T(8,128)(2,1)S(1)}, u32[]{:S(2)}, u32[]{:S(2)}) %all-to-all-start) | async-done | bytes 1048608 | tf_op jit(solution)/shard_map/all_to_all | solution.py:172
  65.6 0.0 collective-permute-done.1.kh_ref.vh_ref
  65.6 1.0 copy-done
  66.7 8.0 %shard_map.59 = bf16[1024,256]{1,0:T(8,128)(2,1)S(1)} custom-call(s32[4]{0:T(128)S(1)} %fusion.tiles_ref, f32[4]{0:T(128)S(1)} %dynamic_slice.3.slopes_ref, s32[1024,1]{1,0:T(8,128)S(1)} %copy-done, bf16[1024,512]{1,0:T(8,128)(2,1)S(1)} %bitcast.11, bf16[1024,512]{1,0:T(8,128)(2,1)S(1)} %bitcast.6, bf16[1024,512]{1,0:T(8,128)(2,1)S(1)} %bitcast.7, ...), custom_call_target="tpu_custom_call" | custom-call | flops 1342177280 | bytes 3145728 | tf_op jit(solution)/shard_map/pallas_call | solution.py:131
  74.7 5.4 %collective-permute-done.kh_ref.vh_ref = bf16[1024,512]{1,0:T(8,128)(2,1)} collective-permute-done((bf16[1024,512]{1,0:T(8,128)(2,1)S(1)}, bf16[1024,512]{1,0:T(8,128)(2,1)}, u32[]{:S(2)}, u32[]{:S(2)}) %collective-permute-start) | collective-permute-done | bytes 1048608 | tf_op jit(solution)/shard_map/ppermute | solution.py:180
  80.1 8.0 %shard_map.57 = bf16[1024,256]{1,0:T(8,128)(2,1)S(1)} custom-call(s32[4]{0:T(128)S(1)} %fusion.tiles_ref, f32[4]{0:T(128)S(1)} %dynamic_slice.3.slopes_ref, s32[1024,1]{1,0:T(8,128)S(1)} %copy-done, bf16[1024,512]{1,0:T(8,128)(2,1)S(1)} %bitcast.12, bf16[1024,512]{1,0:T(8,128)(2,1)S(1)} %bitcast.9, bf16[1024,512]{1,0:T(8,128)(2,1)S(1)} %bitcast.10, ...), custom_call_target="tpu_custom_call" | custom-call | flops 1342177280 | bytes 3145728 | tf_op jit(solution)/shard_map/pallas_call | solution.py:131
  88.2 0.1 pad_maximum_fusion
  88.3 19.6 %all_to_all.20.recv_ref = bf16[8,128,512]{2,1,0:T(8,128)(2,1)S(1)} all-to-all(bf16[8,128,512]{2,1,0:T(8,128)(2,1)S(1)} %bitcast.13), channel_id=1, replica_groups={{0,1,2,3,4,5,6,7},{8,9,10,11,12,13,14,15},{16,17,18,19,20,21,22,23},{24..., dimensions={0} | all-to-all | bytes 2097152 | tf_op jit(solution)/shard_map/all_to_all | solution.py:201
  107.8 1.0 shard_map.60
  (16 shorter events, 0.0 us)
Async XLA Ops:
  0.0 1.2 %copy-start.1 = (bf16[128,4096]{1,0:T(8,128)(2,1)S(1)}, bf16[128,4096]{1,0:T(8,128)(2,1)}, u32[]{:S(2)}) copy-start(bf16[128,4096]{1,0:T(8,128)(2,1)} %refs_0_.5) | copy-start | bytes 3145732
  1.2 1.2 %copy-start.3 = (bf16[128,4096]{1,0:T(8,128)(2,1)S(1)}, bf16[128,4096]{1,0:T(8,128)(2,1)}, u32[]{:S(2)}) copy-start(bf16[128,4096]{1,0:T(8,128)(2,1)} %refs_1_.3) | copy-start | bytes 3145732
  2.5 1.0 copy-start.6
  3.5 4.4 %copy-start.2 = (bf16[128,4096]{1,0:T(8,128)(2,1)S(1)}, bf16[128,4096]{1,0:T(8,128)(2,1)}, u32[]{:S(2)}) copy-start(bf16[128,4096]{1,0:T(8,128)(2,1)} %refs_0_.5) | copy-start | bytes 3145732
  3.5 4.4 %copy-start.4 = (bf16[128,4096]{1,0:T(8,128)(2,1)S(1)}, bf16[128,4096]{1,0:T(8,128)(2,1)}, u32[]{:S(2)}) copy-start(bf16[128,4096]{1,0:T(8,128)(2,1)} %refs_1_.3) | copy-start | bytes 3145732
  3.5 19.8 %all-to-all-start.2 = ((bf16[8,128,512]{2,1,0:T(8,128)(2,1)}), bf16[8,128,512]{2,1,0:T(8,128)(2,1)S(1)}, u32[]{:S(2)}, u32[]{:S(2)}) async-start(bf16[8,128,512]{2,1,0:T(8,128)(2,1)} %copy-done.6), calls=%async_computation.2 | async-start | bytes 2097152 | tf_op jit(solution)/shard_map/all_to_all | solution.py:172
  8.0 1.0 copy-start.5
  9.0 36.6 %copy-start.8 = (bf16[128,4096]{1,0:T(8,128)(2,1)S(1)}, bf16[128,4096]{1,0:T(8,128)(2,1)}, u32[]{:S(2)}) copy-start(bf16[128,4096]{1,0:T(8,128)(2,1)} %refs_0_.3) | copy-start | bytes 3145732
  23.3 18.8 %all-to-all-start.1 = ((bf16[8,128,512]{2,1,0:T(8,128)(2,1)}), bf16[8,128,512]{2,1,0:T(8,128)(2,1)S(1)}, u32[]{:S(2)}, u32[]{:S(2)}) async-start(bf16[8,128,512]{2,1,0:T(8,128)(2,1)} %copy-done.5), calls=%async_computation.1 | async-start | bytes 2097152 | tf_op jit(solution)/shard_map/all_to_all | solution.py:172
  26.9 38.8 %collective-permute-start.1 = (bf16[1024,512]{1,0:T(8,128)(2,1)S(1)}, bf16[1024,512]{1,0:T(8,128)(2,1)}, u32[]{:S(2)}, u32[]{:S(2)}) collective-permute-start(bf16[1024,512]{1,0:T(8,128)(2,1)S(1)} %bitcast.5), channel_id=1, source_target_pairs={{0,8},{1,9},{2,10},{3,11},{4,12},{5,13},{6,14},{7,15},{8,16},{9,17... | collective-permute-start | bytes 3145736 | tf_op jit(solution)/shard_map/ppermute | solution.py:180
  42.1 38.0 %collective-permute-start = (bf16[1024,512]{1,0:T(8,128)(2,1)S(1)}, bf16[1024,512]{1,0:T(8,128)(2,1)}, u32[]{:S(2)}, u32[]{:S(2)}) collective-permute-start(bf16[1024,512]{1,0:T(8,128)(2,1)S(1)} %bitcast.8), channel_id=1, source_target_pairs={{0,8},{1,9},{2,10},{3,11},{4,12},{5,13},{6,14},{7,15},{8,16},{9,17... | collective-permute-start | bytes 3145736 | tf_op jit(solution)/shard_map/ppermute | solution.py:180
  45.7 1.0 copy-start.7
  46.7 3.7 %copy-start.9 = (s32[128]{0:T(128)S(1)}, s32[128]{0:T(128)}, u32[]{:S(2)}) copy-start(s32[128]{0:T(128)} %param.8) | copy-start | bytes 1540
  46.7 5.4 %copy-start.10 = (f32[32]{0:T(128)S(1)}, f32[32]{0:T(128)}, u32[]{:S(2)}) copy-start(f32[32]{0:T(128)} %param.9) | copy-start | bytes 388
  46.7 19.0 %all-to-all-start = ((bf16[8,128,512]{2,1,0:T(8,128)(2,1)}), bf16[8,128,512]{2,1,0:T(8,128)(2,1)S(1)}, u32[]{:S(2)}, u32[]{:S(2)}) async-start(bf16[8,128,512]{2,1,0:T(8,128)(2,1)} %copy-done.7), calls=%async_computation | async-start | bytes 2097152 | tf_op jit(solution)/shard_map/all_to_all | solution.py:172
  65.6 1.0 copy-start

commit v2 on v1

v2 whole, which is shorter than its diff:
```python
import functools
import math

import jax
import jax.numpy as jnp
from jax import lax
from jax.experimental import pallas as pl
from jax.experimental.pallas import tpu as pltpu
from jax.sharding import PartitionSpec as P

AXES = ("outer", "inner")
TILE = 256
NEG_FILL = -1e30
VMEM_BYTES = 60 << 20
LOG2E = math.log2(math.e)
IN_BATCHES = ((2, 0), (2, 0), (0, 4))
OUT_BATCHES = (2, 2)


def copy_all(copies):
    for copy in copies:
        copy.start()
    for copy in copies:
        copy.wait()


def pack_kernel(pieces, count, *refs):
    sources, (out_ref, stage, in_sems, out_sems) = refs[:-4], refs[-4:]
    groups = out_ref.shape[0]
    loads, stores = [], []
    for group in range(groups):
        place, mine = 0, []
        for i, (source, (head, heads)) in enumerate(zip(sources, pieces)):
            mine.append(
                pltpu.make_async_copy(
                    source.at[:, pl.ds((group * count + head) * 128, heads * 128)],
                    stage.at[group, :, pl.ds(place, heads * 128)],
                    in_sems.at[group, i],
                )
            )
            place += heads * 128
        loads.append(mine)
        stores.append(pltpu.make_async_copy(stage.at[group], out_ref.at[group], out_sems.at[group]))
    for mine in loads:
        for load in mine:
            load.start()
    for mine, store in zip(loads, stores):
        for load in mine:
            load.wait()
        store.start()
    for store in stores:
        store.wait()


def pack(sources, pieces, count, groups):
    rows = sources[0].shape[0]
    width = sum(heads for _, heads in pieces) * 128
    shape = (groups, rows, width)
    return pl.pallas_call(
        functools.partial(pack_kernel, pieces, count),
        out_shape=jax.ShapeDtypeStruct(shape, jnp.bfloat16),
        in_specs=[pl.BlockSpec(memory_space=pltpu.HBM)] * len(sources),
        out_specs=pl.BlockSpec(memory_space=pltpu.HBM),
        scratch_shapes=[
            pltpu.VMEM(shape, jnp.bfloat16),
            pltpu.SemaphoreType.DMA((groups, len(sources))),
            pltpu.SemaphoreType.DMA((groups,)),
        ],
        compiler_params=pltpu.CompilerParams(vmem_limit_bytes=VMEM_BYTES),
        cost_estimate=pl.CostEstimate(
            flops=0, bytes_accessed=4 * groups * rows * width, transcendentals=0
        ),
    )(*sources)


def unpack_kernel(count, *refs):
    parts, out_ref = refs[:-1], refs[-1]
    place = 0
    for part in parts:
        groups, _, width = part.shape
        for group in range(groups):
            column = group * count * 128 + place
            out_ref[:, column : column + width] = part[group]
        place += width


def unpack(parts, count):
    groups, rows = parts[0].shape[:2]
    return pl.pallas_call(
        functools.partial(unpack_kernel, count),
        out_shape=jax.ShapeDtypeStruct((rows, groups * count * 128), jnp.bfloat16),
        in_specs=[pl.BlockSpec(memory_space=pltpu.VMEM)] * len(parts),
        out_specs=pl.BlockSpec(memory_space=pltpu.VMEM),
        compiler_params=pltpu.CompilerParams(vmem_limit_bytes=16 << 20),
    )(*parts)


def attend_kernel(
    inv_root, first, q_place, out_place, tiles_ref, slopes_ref, firsts_ref, q_hbm, own_hbm, halo_hbm,
    *refs,
):
    out_hbm, q_all, both_win, value_win, out_all, sems = refs[-6:]
    span = q_all.shape[0]
    heads = q_all.shape[1] // 128
    tiles = span // TILE
    most = tiles + 1
    halves = [pl.ds(0, span), pl.ds(span, span)]
    copies = [
        pltpu.make_async_copy(
            own_hbm.at[:, pl.ds(0, 2 * heads * 128)], both_win.at[halves[1], :], sems.at[0]
        ),
        pltpu.make_async_copy(halo_hbm, both_win.at[halves[0], :], sems.at[1]),
        pltpu.make_async_copy(q_hbm.at[:, pl.ds(q_place * 128, heads * 128)], q_all, sems.at[2]),
    ]
    for copy in copies:
        copy.start()
    for head in range(heads):
        value_win[head, 128:, :] = jnp.ones((16, 2 * span), jnp.bfloat16)
    for copy, half in zip(copies, halves[::-1]):
        copy.wait()
        for head in range(heads):
            columns = slice((heads + head) * 128, (heads + head + 1) * 128)
            value_win[head, :128, half] = both_win[half, columns].T
    copies[2].wait()
    firsts = firsts_ref[...]

    def one_tile(tile, _):
        row = pl.multiple_of(tile * TILE, TILE)
        needed = tiles_ref[tile]
        at = lax.broadcasted_iota(jnp.int32, (128, TILE), 1) + (span + row)
        begin_all = jnp.max(jnp.where(firsts <= at, firsts, 0), axis=0, keepdims=True)

        for count in range(1, most + 1):

            @pl.when(needed == count)
            def _():
                width = count * TILE
                base = pl.multiple_of((tile + tiles + 1 - count) * TILE, TILE)
                begin = begin_all - base
                offset = lax.broadcasted_iota(jnp.int32, (width, TILE), 0)
                distance = (offset - width).astype(jnp.float32)
                key_in = lax.broadcasted_iota(jnp.int32, (TILE, TILE), 0)
                query_in = lax.broadcasted_iota(jnp.int32, (TILE, TILE), 1)
                in_document = offset >= begin
                past = key_in <= query_in
                all_scores = []
                for head in range(heads):
                    columns = slice(head * 128, (head + 1) * 128)
                    all_scores.append(
                        lax.dot_general(
                            both_win[pl.ds(base, width), columns],
                            q_all[pl.ds(row, TILE), columns],
                            (((1,), (1,)), ((), ())),
                            preferred_element_type=jnp.float32,
                        )
                    )
                for head, scores in enumerate(all_scores):
                    slope = slopes_ref[first + head] * LOG2E
                    scores = scores * (inv_root * LOG2E) + slope * distance
                    scores = jnp.where(in_document, scores, NEG_FILL)
                    last = jnp.where(past, scores[width - TILE :], NEG_FILL)
                    if count > 1:
                        scores = jnp.concatenate([scores[: width - TILE], last], axis=0)
                    else:
                        scores = last
                    all_scores[head] = scores
                all_weights = []
                for scores in all_scores:
                    row_max = jnp.max(scores, axis=0, keepdims=True)
                    all_weights.append(jnp.exp2(scores - row_max).astype(jnp.bfloat16))
                for head, weights in enumerate(all_weights):
                    columns = slice(head * 128, (head + 1) * 128)
                    both = lax.dot_general(
                        value_win[head, :, pl.ds(base, width)],
                        weights,
                        (((1,), (0,)), ((), ())),
                        preferred_element_type=jnp.float32,
                    )
                    result = both[:128] * (1.0 / both[128:129])
                    out_all[pl.ds(row, TILE), columns] = result.T.astype(jnp.bfloat16)

        return 0

    lax.fori_loop(0, tiles, one_tile, 0)
    place = pl.ds(out_place * 128, heads * 128)
    copy_all([pltpu.make_async_copy(out_all, out_hbm.at[:, place], sems.at[0])])


def attend(
    tiles_needed, slopes, firsts, queries, own, halo, first, heads, q_place, before, out_heads, out_place
):
    span = queries.shape[0]
    smem = pl.BlockSpec(memory_space=pltpu.SMEM)
    hbm = pl.BlockSpec(memory_space=pltpu.HBM)
    more = [] if before is None else [before]
    return pl.pallas_call(
        functools.partial(attend_kernel, 1.0 / math.sqrt(128), first, q_place, out_place),
        out_shape=jax.ShapeDtypeStruct((span, out_heads * 128), jnp.bfloat16),
        in_specs=[smem, smem, pl.BlockSpec(memory_space=pltpu.VMEM), hbm, hbm, hbm]
        + [pl.BlockSpec(memory_space=pltpu.HBM)] * len(more),
        out_specs=pl.BlockSpec(memory_space=pltpu.HBM),
        input_output_aliases={6: 0} if more else {},
        scratch_shapes=[
            pltpu.VMEM((span, heads * 128), jnp.bfloat16),
            pltpu.VMEM((2 * span, 2 * heads * 128), jnp.bfloat16),
            pltpu.VMEM((heads, 144, 2 * span), jnp.bfloat16),
            pltpu.VMEM((span, heads * 128), jnp.bfloat16),
            pltpu.SemaphoreType.DMA((3,)),
        ],
        compiler_params=pltpu.CompilerParams(vmem_limit_bytes=40 << 20),
        cost_estimate=pl.CostEstimate(
            flops=heads * 4 * span * (span + TILE) * 128,
            bytes_accessed=heads * span * 128 * 12,
            transcendentals=heads * span * (span + TILE),
        ),
    )(tiles_needed, slopes, firsts, queries, own, halo, *more)


def per_device(query_states, key_states, value_states, doc_lengths, slopes):
    rows = query_states.shape[0]
    outer, inner = lax.axis_size("outer"), lax.axis_size("inner")
    groups = 2 * inner
    supers = outer * inner // groups
    span = groups * rows
    count = slopes.shape[0] // groups
    me = lax.axis_index("outer") * inner + lax.axis_index("inner")
    super_index, member = me // groups, me % groups
    index_groups = [[s * groups + m for m in range(groups)] for s in range(supers)]
    onward = [(i, i + groups) for i in range((supers - 1) * groups)]

    def exchange(value):
        got = lax.all_to_all(value, AXES, 0, 0, axis_index_groups=index_groups)
        return got.reshape(span, value.shape[-1])

    own, halo, first_of, queries = [], [], [], {}
    next_kv, next_q = 0, 0
    for kv, q in IN_BATCHES:
        pieces = [(key_states, (next_kv, kv)), (value_states, (next_kv, kv))] * (kv > 0)
        pieces += [(query_states, (next_q, q))] * (q > 0)
        packed = pack([p[0] for p in pieces], tuple(p[1] for p in pieces), count, groups)
        got = exchange(packed)
        if kv:
            own.append(got)
            halo.append(lax.ppermute(got[:, : 2 * kv * 128], AXES, onward))
            first_of.append((next_kv, kv))
        for i in range(q):
            queries[next_q + i] = (got, 2 * kv + i)
        next_kv, next_q = next_kv + kv, next_q + q

    ids = jnp.arange(doc_lengths.shape[0])
    firsts = jnp.sum(jnp.where(ids[:, None] < ids[None, :], doc_lengths[:, None], 0), axis=0)
    firsts = firsts - (super_index - 1) * span
    tiles = span // TILE
    block = jnp.arange(tiles, dtype=jnp.int32)
    starts = jnp.max(jnp.where(firsts[None, :] <= (span + block * TILE)[:, None], firsts[None, :], 0), axis=1)
    needed = block + tiles + 1 - starts // TILE
    my_slopes = lax.dynamic_slice(slopes, (member * count,), (count,))

    outs, done, place, batch = [], None, 0, 0
    for i, (first, heads) in enumerate(first_of):
        asked, q_place = queries[first]
        done = attend(
            needed, my_slopes, firsts[:, None], asked, own[i], halo[i], first, heads, q_place,
            done, OUT_BATCHES[batch], place,
        )
        place += heads
        if place == OUT_BATCHES[batch]:
            done = done.reshape(groups, rows, place * 128)
            outs.append(lax.all_to_all(done, AXES, 0, 0, axis_index_groups=index_groups))
            done, place, batch = None, 0, batch + 1
    return unpack(outs, count)


def solution(mesh):
    tokens = P(AXES, None)
    return jax.shard_map(
        per_device,
        mesh=mesh,
        in_specs=(tokens, tokens, tokens, P(), P()),
        out_specs=tokens,
        check_vma=False,
    )
```

time: 110 us -> 101 us (0.918)
  the two profiles are of different devices: /device:TPU:256 before, /device:TPU:9 now
where the time goes in v2:
time: 101 us; the launch traced here: 100 us
  waiting for transfers between devices  39.7 us (39%)
  starting transfers between devices  22.9 us (23%)
  Pallas kernels  21.3 us (21%)
  blocking collectives  14.3 us (14%)
  local copies, waits for them, and re-layouts  1.63 us (2%)
    all_to_all x3, waiting for transfers between devices, exchange(): got = lax.all_to_all(value, AXES, 0, 0, axis_index_groups=index_groups)  33.1 us
    all_to_all x1, blocking collectives, per_device(): lax.all_to_all(done, AXES, 0, 0, axis_index_groups=index_groups)  14.3 us
    pallas_call x2, Pallas kernels, attend(): pl.pallas_call(functools.partial(attend_kernel, 1.0 / math.sqrt(128), fir...  13.9 us
    all_to_all x3, starting transfers between devices, exchange(): got = lax.all_to_all(value, AXES, 0, 0, axis_index_groups=index_groups)  12.7 us
    ppermute x2, waiting for transfers between devices, per_device(): halo.append(lax.ppermute(got[:, :2 * kv * 128], AXES, onward))  6.67 us
    ppermute x2, starting transfers between devices, per_device(): halo.append(lax.ppermute(got[:, :2 * kv * 128], AXES, onward))  6.43 us
    pallas_call x3, Pallas kernels, pack(): pl.pallas_call(functools.partial(pack_kernel, pieces, count), out_shape=j...  6.34 us
    all_to_all x1, starting transfers between devices, per_device(): lax.all_to_all(done, AXES, 0, 0, axis_index_groups=index_groups)  3.77 us
  transfers between devices with their start and end apart: 6, of which 4 were waited for; matrix products, arithmetic and copies ran while one was open for 0% of the time, Pallas kernels for 18%

profile of v2, /device:TPU:9, one launch (start us, length us, event | category | flops | bytes accessed | tf_op | source)
XLA Modules:
  0.0 100.3 jit_solution(5344666385116331908)
XLA Ops:
  0.0 2.1 %shard_map.56 = bf16[8,128,512]{2,1,0:T(8,128)(2,1)} custom-call(bf16[128,4096]{1,0:T(8,128)(2,1)} %refs_0_.5, bf16[128,4096]{1,0:T(8,128)(2,1)} %refs_1_.3), custom_call_target="tpu_custom_call" | custom-call | bytes 2097152 | tf_op jit(solution)/shard_map/pallas_call | solution.py:59
  2.1 5.0 %all-to-all-start.1 = ((bf16[8,128,512]{2,1,0:T(8,128)(2,1)}), bf16[8,128,512]{2,1,0:T(8,128)(2,1)S(1)}, u32[]{:S(2)}, u32[]{:S(2)}) async-start(bf16[8,128,512]{2,1,0:T(8,128)(2,1)} %shard_map.56), calls=%async_computation.1 | async-start | bytes 2097152 | tf_op jit(solution)/shard_map/all_to_all | solution.py:232
  7.1 2.1 %shard_map.58 = bf16[8,128,512]{2,1,0:T(8,128)(2,1)} custom-call(bf16[128,4096]{1,0:T(8,128)(2,1)} %refs_0_.5, bf16[128,4096]{1,0:T(8,128)(2,1)} %refs_1_.3), custom_call_target="tpu_custom_call" | custom-call | bytes 2097152 | tf_op jit(solution)/shard_map/pallas_call | solution.py:59
  9.2 12.9 %all-to-all-done.1 = bf16[8,128,512]{2,1,0:T(8,128)(2,1)S(1)} async-done(((bf16[8,128,512]{2,1,0:T(8,128)(2,1)}), bf16[8,128,512]{2,1,0:T(8,128)(2,1)S(1)}, u32[]{:S(2)}, u32[]{:S(2)}) %all-to-all-start.1) | async-done | bytes 1048608 | tf_op jit(solution)/shard_map/all_to_all | solution.py:232
  22.1 3.8 %all-to-all-start.3 = ((bf16[8,128,512]{2,1,0:T(8,128)(2,1)}), bf16[8,128,512]{2,1,0:T(8,128)(2,1)S(1)}, u32[]{:S(2)}, u32[]{:S(2)}) async-start(bf16[8,128,512]{2,1,0:T(8,128)(2,1)} %shard_map.58), calls=%async_computation.3 | async-start | bytes 2097152 | tf_op jit(solution)/shard_map/all_to_all | solution.py:232
  25.9 3.2 %collective-permute-start = (bf16[1024,512]{1,0:T(8,128)(2,1)S(1)}, bf16[1024,512]{1,0:T(8,128)(2,1)}, u32[]{:S(2)}, u32[]{:S(2)}) collective-permute-start(bf16[1024,512]{1,0:T(8,128)(2,1)S(1)} %bitcast.7), channel_id=1, source_target_pairs={{0,8},{1,9},{2,10},{3,11},{4,12},{5,13},{6,14},{7,15},{8,16},{9,17... | collective-permute-start | bytes 3145736 | tf_op jit(solution)/shard_map/ppermute | solution.py:244
  29.2 2.1 %shard_map.55 = bf16[8,128,512]{2,1,0:T(8,128)(2,1)} custom-call(bf16[128,4096]{1,0:T(8,128)(2,1)} %refs_0_.3), custom_call_target="tpu_custom_call" | custom-call | bytes 2097152 | tf_op jit(solution)/shard_map/pallas_call | solution.py:59
  31.3 0.0 copy-start.1
  31.3 9.7 %all-to-all-done.3 = bf16[8,128,512]{2,1,0:T(8,128)(2,1)S(1)} async-done(((bf16[8,128,512]{2,1,0:T(8,128)(2,1)}), bf16[8,128,512]{2,1,0:T(8,128)(2,1)S(1)}, u32[]{:S(2)}, u32[]{:S(2)}) %all-to-all-start.3) | async-done | bytes 1048608 | tf_op jit(solution)/shard_map/all_to_all | solution.py:232
  40.9 3.8 %all-to-all-start = ((bf16[8,128,512]{2,1,0:T(8,128)(2,1)}), bf16[8,128,512]{2,1,0:T(8,128)(2,1)S(1)}, u32[]{:S(2)}, u32[]{:S(2)}) async-start(bf16[8,128,512]{2,1,0:T(8,128)(2,1)} %shard_map.55), calls=%async_computation | async-start | bytes 2097152 | tf_op jit(solution)/shard_map/all_to_all | solution.py:232
  44.8 0.0 copy-done.1
  44.8 0.1 select_reduce_fusion
  44.9 3.2 %collective-permute-start.1 = (bf16[1024,512]{1,0:T(8,128)(2,1)S(1)}, bf16[1024,512]{1,0:T(8,128)(2,1)}, u32[]{:S(2)}, u32[]{:S(2)}) collective-permute-start(bf16[1024,512]{1,0:T(8,128)(2,1)S(1)} %bitcast.9), channel_id=1, source_target_pairs={{0,8},{1,9},{2,10},{3,11},{4,12},{5,13},{6,14},{7,15},{8,16},{9,17... | collective-permute-start | bytes 3145736 | tf_op jit(solution)/shard_map/ppermute | solution.py:244
  48.2 0.1 copy.8.firsts_ref
  48.3 0.0 copy-start.2
  48.3 0.6 copy-done.2
  48.9 0.1 dynamic_slice.3.slopes_ref
  49.0 0.2 select_reduce_fusion.1
  49.2 10.6 %all-to-all-done = bf16[8,128,512]{2,1,0:T(8,128)(2,1)S(1)} async-done(((bf16[8,128,512]{2,1,0:T(8,128)(2,1)}), bf16[8,128,512]{2,1,0:T(8,128)(2,1)S(1)}, u32[]{:S(2)}, u32[]{:S(2)}) %all-to-all-start) | async-done | bytes 1048608 | tf_op jit(solution)/shard_map/all_to_all | solution.py:232
  59.8 0.0 collective-permute-done.halo_hbm
  59.8 6.9 %shard_map.57 = bf16[1024,256]{1,0:T(8,128)(2,1)S(1)} custom-call(s32[4]{0:T(128)S(1)} %fusion.tiles_ref, f32[4]{0:T(128)S(1)} %dynamic_slice.3.slopes_ref, s32[128,1]{1,0:T(8,128)S(1)} %copy.8.firsts_ref, bf16[1024,512]{1,0:T(8,128)(2,1)S(1)} %bitcast.11, bf16[1024,512]{1,0:T(8,128)(2,1)S(1)} %bitcast.8, bf16[1024,512]{1,0:T(8,128)(2,1)} %collective-permute-done.halo_hbm), custom_call_target="tpu_custom_call" | custom-call | flops 1342177280 | bytes 3145728 | tf_op jit(solution)/shard_map/pallas_call | solution.py:196
  66.7 0.0 copy-start
  66.7 0.8 copy-done
  67.5 3.8 %all-to-all-start.2 = ((bf16[8,128,256]{2,1,0:T(8,128)(2,1)}), bf16[8,128,256]{2,1,0:T(8,128)(2,1)S(1)}, u32[]{:S(2)}, u32[]{:S(2)}) async-start(bf16[8,128,256]{2,1,0:T(8,128)(2,1)} %bitcast.13), calls=%async_computation.2 | async-start | bytes 1048576 | tf_op jit(solution)/shard_map/all_to_all | solution.py:269
  71.3 6.7 %collective-permute-done.1.halo_hbm = bf16[1024,512]{1,0:T(8,128)(2,1)} collective-permute-done((bf16[1024,512]{1,0:T(8,128)(2,1)S(1)}, bf16[1024,512]{1,0:T(8,128)(2,1)}, u32[]{:S(2)}, u32[]{:S(2)}) %collective-permute-start.1) | collective-permute-done | bytes 1048608 | tf_op jit(solution)/shard_map/ppermute | solution.py:244
  77.9 6.9 %shard_map.59 = bf16[1024,256]{1,0:T(8,128)(2,1)S(1)} custom-call(s32[4]{0:T(128)S(1)} %fusion.tiles_ref, f32[4]{0:T(128)S(1)} %dynamic_slice.3.slopes_ref, s32[128,1]{1,0:T(8,128)S(1)} %copy.8.firsts_ref, bf16[1024,512]{1,0:T(8,128)(2,1)S(1)} %bitcast.12, bf16[1024,512]{1,0:T(8,128)(2,1)S(1)} %bitcast.10, bf16[1024,512]{1,0:T(8,128)(2,1)} %collective-permute-done.1.halo_hbm), custom_call_target="tpu_custom_call" | custom-call | flops 1342177280 | bytes 3145728 | tf_op jit(solution)/shard_map/pallas_call | solution.py:196
  84.9 0.0 all-to-all-done.2.refs_0_
  84.9 14.3 %all_to_all.25.refs_1_ = bf16[8,128,256]{2,1,0:T(8,128)(2,1)S(1)} all-to-all(bf16[8,128,256]{2,1,0:T(8,128)(2,1)S(1)} %bitcast.14), channel_id=1, replica_groups={{0,1,2,3,4,5,6,7},{8,9,10,11,12,13,14,15},{16,17,18,19,20,21,22,23},{24..., dimensions={0} | all-to-all | bytes 1048576 | tf_op jit(solution)/shard_map/all_to_all | solution.py:269
  99.2 1.1 %shard_map.60 = bf16[128,4096]{1,0:T(8,128)(2,1)} custom-call(bf16[8,128,256]{2,1,0:T(8,128)(2,1)S(1)} %all-to-all-done.2.refs_0_, bf16[8,128,256]{2,1,0:T(8,128)(2,1)S(1)} %all_to_all.25.refs_1_), custom_call_target="tpu_custom_call" | custom-call | tf_op jit(solution)/shard_map/pallas_call | solution.py:89
  (4 shorter events, 0.0 us)
Async XLA Ops:
  2.1 20.0 %all-to-all-start.1 = ((bf16[8,128,512]{2,1,0:T(8,128)(2,1)}), bf16[8,128,512]{2,1,0:T(8,128)(2,1)S(1)}, u32[]{:S(2)}, u32[]{:S(2)}) async-start(bf16[8,128,512]{2,1,0:T(8,128)(2,1)} %shard_map.56), calls=%async_computation.1 | async-start | bytes 2097152 | tf_op jit(solution)/shard_map/all_to_all | solution.py:232
  22.1 18.8 %all-to-all-start.3 = ((bf16[8,128,512]{2,1,0:T(8,128)(2,1)}), bf16[8,128,512]{2,1,0:T(8,128)(2,1)S(1)}, u32[]{:S(2)}, u32[]{:S(2)}) async-start(bf16[8,128,512]{2,1,0:T(8,128)(2,1)} %shard_map.58), calls=%async_computation.3 | async-start | bytes 2097152 | tf_op jit(solution)/shard_map/all_to_all | solution.py:232
  25.9 33.8 %collective-permute-start = (bf16[1024,512]{1,0:T(8,128)(2,1)S(1)}, bf16[1024,512]{1,0:T(8,128)(2,1)}, u32[]{:S(2)}, u32[]{:S(2)}) collective-permute-start(bf16[1024,512]{1,0:T(8,128)(2,1)S(1)} %bitcast.7), channel_id=1, source_target_pairs={{0,8},{1,9},{2,10},{3,11},{4,12},{5,13},{6,14},{7,15},{8,16},{9,17... | collective-permute-start | bytes 3145736 | tf_op jit(solution)/shard_map/ppermute | solution.py:244
  31.3 13.5 %copy-start.1 = (s32[128]{0:T(128)S(1)}, s32[128]{0:T(128)}, u32[]{:S(2)}) copy-start(s32[128]{0:T(128)} %param.8) | copy-start | bytes 1540
  40.9 18.8 %all-to-all-start = ((bf16[8,128,512]{2,1,0:T(8,128)(2,1)}), bf16[8,128,512]{2,1,0:T(8,128)(2,1)S(1)}, u32[]{:S(2)}, u32[]{:S(2)}) async-start(bf16[8,128,512]{2,1,0:T(8,128)(2,1)} %shard_map.55), calls=%async_computation | async-start | bytes 2097152 | tf_op jit(solution)/shard_map/all_to_all | solution.py:232
  44.9 33.0 %collective-permute-start.1 = (bf16[1024,512]{1,0:T(8,128)(2,1)S(1)}, bf16[1024,512]{1,0:T(8,128)(2,1)}, u32[]{:S(2)}, u32[]{:S(2)}) collective-permute-start(bf16[1024,512]{1,0:T(8,128)(2,1)S(1)} %bitcast.9), channel_id=1, source_target_pairs={{0,8},{1,9},{2,10},{3,11},{4,12},{5,13},{6,14},{7,15},{8,16},{9,17... | collective-permute-start | bytes 3145736 | tf_op jit(solution)/shard_map/ppermute | solution.py:244
  48.3 0.7 copy-start.2
  66.7 0.8 copy-start
  67.5 17.4 %all-to-all-start.2 = ((bf16[8,128,256]{2,1,0:T(8,128)(2,1)}), bf16[8,128,256]{2,1,0:T(8,128)(2,1)S(1)}, u32[]{:S(2)}, u32[]{:S(2)}) async-start(bf16[8,128,256]{2,1,0:T(8,128)(2,1)} %bitcast.13), calls=%async_computation.2 | async-start | bytes 1048576 | tf_op jit(solution)/shard_map/all_to_all | solution.py:269

commit v3 on v2

--- a/solution.py
+++ b/solution.py
@@ -14,7 +14,6 @@
 VMEM_BYTES = 60 << 20
 LOG2E = math.log2(math.e)
 IN_BATCHES = ((2, 0), (2, 0), (0, 4))
-OUT_BATCHES = (2, 2)
 
 
 def copy_all(copies):
@@ -96,32 +95,30 @@
 
 
 def attend_kernel(
-    inv_root, first, q_place, out_place, tiles_ref, slopes_ref, firsts_ref, q_hbm, own_hbm, halo_hbm,
-    *refs,
+    inv_root, first, q_place, tiles_ref, slopes_ref, firsts_ref, q_ref, own_ref, halo_hbm,
+    out_ref, key_win, value_win, stage, sems,
 ):
-    out_hbm, q_all, both_win, value_win, out_all, sems = refs[-6:]
-    span = q_all.shape[0]
-    heads = q_all.shape[1] // 128
+    span = q_ref.shape[0]
+    heads = out_ref.shape[1] // 128
     tiles = span // TILE
     most = tiles + 1
-    halves = [pl.ds(0, span), pl.ds(span, span)]
+    wide = heads * 128
+    before, mine = pl.ds(0, span), pl.ds(span, span)
     copies = [
-        pltpu.make_async_copy(
-            own_hbm.at[:, pl.ds(0, 2 * heads * 128)], both_win.at[halves[1], :], sems.at[0]
-        ),
-        pltpu.make_async_copy(halo_hbm, both_win.at[halves[0], :], sems.at[1]),
-        pltpu.make_async_copy(q_hbm.at[:, pl.ds(q_place * 128, heads * 128)], q_all, sems.at[2]),
+        pltpu.make_async_copy(halo_hbm.at[:, pl.ds(wide, wide)], stage, sems.at[0]),
+        pltpu.make_async_copy(halo_hbm.at[:, pl.ds(0, wide)], key_win.at[before, :], sems.at[1]),
     ]
     for copy in copies:
         copy.start()
+    key_win[mine, :] = own_ref[:, :wide]
     for head in range(heads):
+        columns = slice(head * 128, (head + 1) * 128)
         value_win[head, 128:, :] = jnp.ones((16, 2 * span), jnp.bfloat16)
-    for copy, half in zip(copies, halves[::-1]):
-        copy.wait()
-        for head in range(heads):
-            columns = slice((heads + head) * 128, (heads + head + 1) * 128)
-            value_win[head, :128, half] = both_win[half, columns].T
-    copies[2].wait()
+        value_win[head, :128, mine] = own_ref[:, wide + head * 128 : wide + (head + 1) * 128].T
+    copies[0].wait()
+    for head in range(heads):
+        value_win[head, :128, before] = stage[:, head * 128 : (head + 1) * 128].T
+    copies[1].wait()
     firsts = firsts_ref[...]
 
     def one_tile(tile, _):
@@ -148,8 +145,8 @@
                     columns = slice(head * 128, (head + 1) * 128)
                     all_scores.append(
                         lax.dot_general(
-                            both_win[pl.ds(base, width), columns],
-                            q_all[pl.ds(row, TILE), columns],
+                            key_win[pl.ds(base, width), columns],
+                            q_ref[pl.ds(row, TILE), pl.ds((q_place + head) * 128, 128)],
                             (((1,), (1,)), ((), ())),
                             preferred_element_type=jnp.float32,
                         )
@@ -177,43 +174,260 @@
                         preferred_element_type=jnp.float32,
                     )
                     result = both[:128] * (1.0 / both[128:129])
-                    out_all[pl.ds(row, TILE), columns] = result.T.astype(jnp.bfloat16)
+                    out_ref[pl.ds(row, TILE), columns] = result.T.astype(jnp.bfloat16)
 
         return 0
 
     lax.fori_loop(0, tiles, one_tile, 0)
-    place = pl.ds(out_place * 128, heads * 128)
-    copy_all([pltpu.make_async_copy(out_all, out_hbm.at[:, place], sems.at[0])])
-
-
-def attend(
-    tiles_needed, slopes, firsts, queries, own, halo, first, heads, q_place, before, out_heads, out_place
-):
+
+
+def attend(tiles_needed, slopes, firsts, queries, own, halo, first, heads, q_place):
     span = queries.shape[0]
     smem = pl.BlockSpec(memory_space=pltpu.SMEM)
-    hbm = pl.BlockSpec(memory_space=pltpu.HBM)
-    more = [] if before is None else [before]
-    return pl.pallas_call(
-        functools.partial(attend_kernel, 1.0 / math.sqrt(128), first, q_place, out_place),
-        out_shape=jax.ShapeDtypeStruct((span, out_heads * 128), jnp.bfloat16),
-        in_specs=[smem, smem, pl.BlockSpec(memory_space=pltpu.VMEM), hbm, hbm, hbm]
-        + [pl.BlockSpec(memory_space=pltpu.HBM)] * len(more),
-        out_specs=pl.BlockSpec(memory_space=pltpu.HBM),
-        input_output_aliases={6: 0} if more else {},
+    vmem = pl.BlockSpec(memory_space=pltpu.VMEM)
+    return pl.pallas_call(
+        functools.partial(attend_kernel, 1.0 / math.sqrt(128), first, q_place),
+        out_shape=jax.ShapeDtypeStruct((span, heads * 128), jnp.bfloat16),
+        in_specs=[smem, smem, vmem, vmem, vmem, pl.BlockSpec(memory_space=pltpu.HBM)],
+        out_specs=vmem,
         scratch_shapes=[
-            pltpu.VMEM((span, heads * 128), jnp.bfloat16),
-            pltpu.VMEM((2 * span, 2 * heads * 128), jnp.bfloat16),
+            pltpu.VMEM((2 * span, heads * 128), jnp.bfloat16),
             pltpu.VMEM((heads, 144, 2 * span), jnp.bfloat16),
             pltpu.VMEM((span, heads * 128), jnp.bfloat16),
-            pltpu.SemaphoreType.DMA((3,)),
+            pltpu.SemaphoreType.DMA((2,)),
         ],
-        compiler_params=pltpu.CompilerParams(vmem_limit_bytes=40 << 20),
+        compiler_params=pltpu.CompilerParams(vmem_limit_bytes=32 << 20),
         cost_estimate=pl.CostEstimate(
             flops=heads * 4 * span * (span + TILE) * 128,
             bytes_accessed=heads * span * 128 * 12,
             transcendentals=heads * span * (span + TILE),
         ),
-    )(tiles_needed, slopes, firsts, queries, own, halo, *more)
+    )(tiles_needed, slopes, firsts, queries, own, halo)
+
+
+def own_kernel(
+    inv_root, first, q_place, tiles_ref, slopes_ref, firsts_ref, q_ref, own_ref, earlier_ref,
+    part_ref, value_win,
+):
+    span = q_ref.shape[0]
+    heads = part_ref.shape[0]
+    tiles = span // TILE
+    wide = heads * 128
+    for head in range(heads):
+        value_win[head, 128:, :] = jnp.ones((16, span), jnp.bfloat16)
+        value_win[head, :128, :] = own_ref[:, wide + head * 128 : wide + (head + 1) * 128].T
+    firsts = firsts_ref[...]
+
+    def one_tile(tile, _):
+        row = pl.multiple_of(tile * TILE, TILE)
+        needed = jnp.minimum(tiles_ref[tile], tile + 1)
+        at = lax.broadcasted_iota(jnp.int32, (128, TILE), 1) + (span + row)
+        begin_all = jnp.max(jnp.where(firsts <= at, firsts, 0), axis=0, keepdims=True)
+
+        for count in range(1, tiles + 1):
+
+            @pl.when(needed == count)
+            def _():
+                width = count * TILE
+                base = pl.multiple_of((tile + 1 - count) * TILE, TILE)
+                begin = begin_all - span - base
+                offset = lax.broadcasted_iota(jnp.int32, (width, TILE), 0)
+                distance = (offset - width).astype(jnp.float32)
+                key_in = lax.broadcasted_iota(jnp.int32, (TILE, TILE), 0)
+                query_in = lax.broadcasted_iota(jnp.int32, (TILE, TILE), 1)
+                in_document = offset >= begin
+                past = key_in <= query_in
+                all_scores = []
+                for head in range(heads):
+                    all_scores.append(
+                        lax.dot_general(
+                            own_ref[pl.ds(base, width), head * 128 : (head + 1) * 128],
+                            q_ref[pl.ds(row, TILE), pl.ds((q_place + head) * 128, 128)],
+                            (((1,), (1,)), ((), ())),
+                            preferred_element_type=jnp.float32,
+                        )
+                    )
+                for head, scores in enumerate(all_scores):
+                    slope = slopes_ref[first + head] * LOG2E
+                    scores = scores * (inv_root * LOG2E) + slope * distance
+                    scores = jnp.where(in_document, scores, NEG_FILL)
+                    last = jnp.where(past, scores[width - TILE :], NEG_FILL)
+                    if count > 1:
+                        scores = jnp.concatenate([scores[: width - TILE], last], axis=0)
+                    else:
+                        scores = last
+                    all_scores[head] = scores
+                tops = [jnp.max(scores, axis=0, keepdims=True) for scores in all_scores]
+                all_weights = [
+                    jnp.exp2(scores - top).astype(jnp.bfloat16)
+                    for scores, top in zip(all_scores, tops)
+                ]
+                for head, weights in enumerate(all_weights):
+                    both = lax.dot_general(
+                        value_win[head, :, pl.ds(base, width)],
+                        weights,
+                        (((1,), (0,)), ((), ())),
+                        preferred_element_type=jnp.float32,
+                    )
+                    part_ref[head, :136, pl.ds(row, TILE)] = both[:136]
+                    part_ref[head, 136:, pl.ds(row, TILE)] = jnp.broadcast_to(tops[head], (8, TILE))
+
+        return 0
+
+    lax.fori_loop(0, tiles, one_tile, 0)
+
+
+def attend_own(tiles_needed, slopes, firsts, queries, own, earlier, first, heads, q_place):
+    span = queries.shape[0]
+    smem = pl.BlockSpec(memory_space=pltpu.SMEM)
+    vmem = pl.BlockSpec(memory_space=pltpu.VMEM)
+    return pl.pallas_call(
+        functools.partial(own_kernel, 1.0 / math.sqrt(128), first, q_place),
+        out_shape=jax.ShapeDtypeStruct((heads, 144, span), jnp.float32),
+        in_specs=[smem, smem, vmem, vmem, vmem, pl.BlockSpec(memory_space=pl.ANY)],
+        out_specs=vmem,
+        scratch_shapes=[pltpu.VMEM((heads, 144, span), jnp.bfloat16)],
+        compiler_params=pltpu.CompilerParams(vmem_limit_bytes=32 << 20),
+        cost_estimate=pl.CostEstimate(
+            flops=heads * 2 * span * (span + TILE) * 128,
+            bytes_accessed=heads * span * 128 * 10,
+            transcendentals=heads * span * (span + TILE) // 2,
+        ),
+    )(tiles_needed, slopes, firsts, queries, own, earlier)
+
+
+def halo_kernel(
+    inv_root, first, q_place, tiles_ref, slopes_ref, firsts_ref, q_ref, part_ref, halo_hbm,
+    out_ref, key_win, value_win, stage, sems,
+):
+    span = q_ref.shape[0]
+    heads = part_ref.shape[0]
+    tiles = span // TILE
+    wide = heads * 128
+    copies = [
+        pltpu.make_async_copy(halo_hbm.at[:, pl.ds(wide, wide)], stage, sems.at[0]),
+        pltpu.make_async_copy(halo_hbm.at[:, pl.ds(0, wide)], key_win, sems.at[1]),
+    ]
+    for copy in copies:
+        copy.start()
+    for head in range(heads):
+        value_win[head, 128:, :] = jnp.ones((16, span), jnp.bfloat16)
+    copies[0].wait()
+    for head in range(heads):
+        value_win[head, :128, :] = stage[:, head * 128 : (head + 1) * 128].T
+    copies[1].wait()
+    firsts = firsts_ref[...]
+
+    def one_tile(tile, _):
+        row = pl.multiple_of(tile * TILE, TILE)
+        needed = tiles_ref[tile] - (tile + 1)
+        at = lax.broadcasted_iota(jnp.int32, (128, TILE), 1) + (span + row)
+        begin_all = jnp.max(jnp.where(firsts <= at, firsts, 0), axis=0, keepdims=True)
+        ahead = ((tile + 1) * TILE).astype(jnp.float32)
+
+        def finish(head, sums, total):
+            columns = slice(head * 128, (head + 1) * 128)
+            result = sums * (1.0 / total)
+            out_ref[pl.ds(row, TILE), columns] = result.T.astype(jnp.bfloat16)
+
+        @pl.when(needed <= 0)
+        def _():
+            for head in range(heads):
+                finish(
+                    head,
+                    part_ref[head, :128, pl.ds(row, TILE)],
+                    part_ref[head, 128:129, pl.ds(row, TILE)],
+                )
+
+        for count in range(1, tiles + 1):
+
+            @pl.when(needed == count)
+            def _():
+                width = count * TILE
+                base = span - width
+                offset = lax.broadcasted_iota(jnp.int32, (width, TILE), 0)
+                distance = (offset - width).astype(jnp.float32) - ahead
+                in_document = offset >= begin_all - base
+                all_scores = []
+                for head in range(heads):
+                    all_scores.append(
+                        lax.dot_general(
+                            key_win[base:, head * 128 : (head + 1) * 128],
+                            q_ref[pl.ds(row, TILE), pl.ds((q_place + head) * 128, 128)],
+                            (((1,), (1,)), ((), ())),
+                            preferred_element_type=jnp.float32,
+                        )
+                    )
+                for head, scores in enumerate(all_scores):
+                    slope = slopes_ref[first + head] * LOG2E
+                    scores = scores * (inv_root * LOG2E) + slope * distance
+                    all_scores[head] = jnp.where(in_document, scores, NEG_FILL)
+                olds = [part_ref[head, 136:137, pl.ds(row, TILE)] for head in range(heads)]
+                tops = [
+                    jnp.maximum(old, jnp.max(scores, axis=0, keepdims=True))
+                    for old, scores in zip(olds, all_scores)
+                ]
+                all_weights = [
+                    jnp.exp2(scores - top).astype(jnp.bfloat16)
+                    for scores, top in zip(all_scores, tops)
+                ]
+                for head, weights in enumerate(all_weights):
+                    both = lax.dot_general(
+                        value_win[head, :, base:],
+                        weights,
+                        (((1,), (0,)), ((), ())),
+                        preferred_element_type=jnp.float32,
+                    )
+                    rescale = jnp.exp2(olds[head] - tops[head])
+                    finish(
+                        head,
+                        both[:128] + rescale * part_ref[head, :128, pl.ds(row, TILE)],
+                        both[128:129] + rescale * part_ref[head, 128:129, pl.ds(row, TILE)],
+                    )
+
+        return 0
+
+    lax.fori_loop(0, tiles, one_tile, 0)
+
+
+def attend_halo(tiles_needed, slopes, firsts, queries, part, halo, first, heads, q_place):
+    span = queries.shape[0]
+    smem = pl.BlockSpec(memory_space=pltpu.SMEM)
+    vmem = pl.BlockSpec(memory_space=pltpu.VMEM)
+    return pl.pallas_call(
+        functools.partial(halo_kernel, 1.0 / math.sqrt(128), first, q_place),
+        out_shape=jax.ShapeDtypeStruct((span, heads * 128), jnp.bfloat16),
+        in_specs=[smem, smem, vmem, vmem, vmem, pl.BlockSpec(memory_space=pltpu.HBM)],
+        out_specs=vmem,
+        scratch_shapes=[
+            pltpu.VMEM((span, heads * 128), jnp.bfloat16),
+            pltpu.VMEM((heads, 144, span), jnp.bfloat16),
+            pltpu.VMEM((span, heads * 128), jnp.bfloat16),
+            pltpu.SemaphoreType.DMA((2,)),
+        ],
+        compiler_params=pltpu.CompilerParams(vmem_limit_bytes=32 << 20),
+        cost_estimate=pl.CostEstimate(
+            flops=heads * 2 * span * (span + TILE) * 128,
+            bytes_accessed=heads * span * 128 * 10,
+            transcendentals=heads * span * (span + TILE) // 2,
+        ),
+    )(tiles_needed, slopes, firsts, queries, part, halo)
+
+
+def follow_kernel(value_ref, earlier_ref, out_ref):
+    pass
+
+
+def follow(value, earlier):
+    anywhere = pl.BlockSpec(memory_space=pl.ANY)
+    return pl.pallas_call(
+        follow_kernel,
+        out_shape=jax.ShapeDtypeStruct(value.shape, value.dtype),
+        in_specs=[anywhere, anywhere],
+        out_specs=anywhere,
+        input_output_aliases={0: 0},
+        compiler_params=pltpu.CompilerParams(vmem_limit_bytes=1 << 20),
+    )(value, earlier)
 
 
 def per_device(query_states, key_states, value_states, doc_lengths, slopes):
@@ -256,18 +470,19 @@
     needed = block + tiles + 1 - starts // TILE
     my_slopes = lax.dynamic_slice(slopes, (member * count,), (count,))
 
-    outs, done, place, batch = [], None, 0, 0
+    outs = []
     for i, (first, heads) in enumerate(first_of):
         asked, q_place = queries[first]
-        done = attend(
-            needed, my_slopes, firsts[:, None], asked, own[i], halo[i], first, heads, q_place,
-            done, OUT_BATCHES[batch], place,
-        )
-        place += heads
-        if place == OUT_BATCHES[batch]:
-            done = done.reshape(groups, rows, place * 128)
-            outs.append(lax.all_to_all(done, AXES, 0, 0, axis_index_groups=index_groups))
-            done, place, batch = None, 0, batch + 1
+        about = (needed, my_slopes, firsts[:, None], asked)
+        if i == 0:
+            done = attend(*about, own[i], halo[i], first, heads, q_place)
+        else:
+            part = attend_own(*about, own[i], own[i], first, heads, q_place)
+            done = attend_halo(*about, part, halo[i], first, heads, q_place)
+        sent = done.reshape(groups, rows, heads * 128)
+        if outs:
+            sent = follow(sent, outs[-1])
+        outs.append(lax.all_to_all(sent, AXES, 0, 0, axis_index_groups=index_groups))
     return unpack(outs, count)
 
 

time: 101 us -> 99.1 us (0.981)
  the two profiles are of different devices: /device:TPU:9 before, /device:TPU:256 now
where the time goes in v3:
time: 99.1 us; the launch traced here: 98.1 us
  waiting for transfers between devices  38.4 us (39%)
  Pallas kernels  22.4 us (23%)
  starting transfers between devices  21.9 us (22%)
  blocking collectives  13.9 us (14%)
    all_to_all x3, waiting for transfers between devices, exchange(): got = lax.all_to_all(value, AXES, 0, 0, axis_index_groups=index_groups)  34.1 us
    all_to_all x1, blocking collectives, per_device(): lax.all_to_all(sent, AXES, 0, 0, axis_index_groups=index_groups)  13.9 us
    all_to_all x3, starting transfers between devices, exchange(): got = lax.all_to_all(value, AXES, 0, 0, axis_index_groups=index_groups)  11.4 us
    ppermute x2, starting transfers between devices, per_device(): halo.append(lax.ppermute(got[:, :2 * kv * 128], AXES, onward))  6.96 us
    pallas_call x1, Pallas kernels, attend(): pl.pallas_call(functools.partial(attend_kernel, 1.0 / math.sqrt(128), fir...  6.67 us
    pallas_call x3, Pallas kernels, pack(): pl.pallas_call(functools.partial(pack_kernel, pieces, count), out_shape=j...  6.34 us
    pallas_call x1, Pallas kernels, attend_halo(): pl.pallas_call(functools.partial(halo_kernel, 1.0 / math.sqrt(128), first...  4.45 us
    ppermute x2, waiting for transfers between devices, per_device(): halo.append(lax.ppermute(got[:, :2 * kv * 128], AXES, onward))  4.33 us
  transfers between devices with their start and end apart: 6, of which 4 were waited for; matrix products, arithmetic and copies ran while one was open for 1% of the time, Pallas kernels for 20%

profile of v3, /device:TPU:256, one launch (start us, length us, event | category | flops | bytes accessed | tf_op | source)
XLA Modules:
  0.0 98.1 jit_solution(2215499299781827735)
XLA Ops:
  0.0 2.1 %shard_map.56 = bf16[8,128,512]{2,1,0:T(8,128)(2,1)} custom-call(bf16[128,4096]{1,0:T(8,128)(2,1)} %refs_0_.5, bf16[128,4096]{1,0:T(8,128)(2,1)} %refs_1_.3), custom_call_target="tpu_custom_call" | custom-call | bytes 2097152 | tf_op jit(solution)/shard_map/pallas_call | solution.py:58
  2.1 4.3 %all-to-all-start.1 = ((bf16[8,128,512]{2,1,0:T(8,128)(2,1)}), bf16[8,128,512]{2,1,0:T(8,128)(2,1)S(1)}, u32[]{:S(2)}, u32[]{:S(2)}) async-start(bf16[8,128,512]{2,1,0:T(8,128)(2,1)} %shard_map.56), calls=%async_computation.1 | async-start | bytes 2097152 | tf_op jit(solution)/shard_map/all_to_all | solution.py:446
  6.4 2.1 %shard_map.58 = bf16[8,128,512]{2,1,0:T(8,128)(2,1)} custom-call(bf16[128,4096]{1,0:T(8,128)(2,1)} %refs_0_.5, bf16[128,4096]{1,0:T(8,128)(2,1)} %refs_1_.3), custom_call_target="tpu_custom_call" | custom-call | bytes 2097152 | tf_op jit(solution)/shard_map/pallas_call | solution.py:58
  8.6 13.2 %all-to-all-done.1 = bf16[8,128,512]{2,1,0:T(8,128)(2,1)S(1)} async-done(((bf16[8,128,512]{2,1,0:T(8,128)(2,1)}), bf16[8,128,512]{2,1,0:T(8,128)(2,1)S(1)}, u32[]{:S(2)}, u32[]{:S(2)}) %all-to-all-start.1) | async-done | bytes 1048608 | tf_op jit(solution)/shard_map/all_to_all | solution.py:446
  21.8 3.6 %all-to-all-start.3 = ((bf16[8,128,512]{2,1,0:T(8,128)(2,1)}), bf16[8,128,512]{2,1,0:T(8,128)(2,1)S(1)}, u32[]{:S(2)}, u32[]{:S(2)}) async-start(bf16[8,128,512]{2,1,0:T(8,128)(2,1)} %shard_map.58), calls=%async_computation.3 | async-start | bytes 2097152 | tf_op jit(solution)/shard_map/all_to_all | solution.py:446
  25.3 3.5 %collective-permute-start = (bf16[1024,512]{1,0:T(8,128)(2,1)S(1)}, bf16[1024,512]{1,0:T(8,128)(2,1)}, u32[]{:S(2)}, u32[]{:S(2)}) collective-permute-start(bf16[1024,512]{1,0:T(8,128)(2,1)S(1)} %bitcast.14), channel_id=1, source_target_pairs={{0,8},{1,9},{2,10},{3,11},{4,12},{5,13},{6,14},{7,15},{8,16},{9,17... | collective-permute-start | bytes 3145736 | tf_op jit(solution)/shard_map/ppermute | solution.py:458
  28.8 2.1 %shard_map.55 = bf16[8,128,512]{2,1,0:T(8,128)(2,1)} custom-call(bf16[128,4096]{1,0:T(8,128)(2,1)} %refs_0_.3), custom_call_target="tpu_custom_call" | custom-call | bytes 2097152 | tf_op jit(solution)/shard_map/pallas_call | solution.py:58
  30.9 0.0 copy-start.1
  31.0 0.0 copy-start.2
  31.0 9.7 %all-to-all-done.3 = bf16[8,128,512]{2,1,0:T(8,128)(2,1)S(1)} async-done(((bf16[8,128,512]{2,1,0:T(8,128)(2,1)}), bf16[8,128,512]{2,1,0:T(8,128)(2,1)S(1)}, u32[]{:S(2)}, u32[]{:S(2)}) %all-to-all-start.3) | async-done | bytes 1048608 | tf_op jit(solution)/shard_map/all_to_all | solution.py:446
  40.6 3.6 %all-to-all-start = ((bf16[8,128,512]{2,1,0:T(8,128)(2,1)}), bf16[8,128,512]{2,1,0:T(8,128)(2,1)S(1)}, u32[]{:S(2)}, u32[]{:S(2)}) async-start(bf16[8,128,512]{2,1,0:T(8,128)(2,1)} %shard_map.55), calls=%async_computation | async-start | bytes 2097152 | tf_op jit(solution)/shard_map/all_to_all | solution.py:446
  44.2 0.0 copy-done.1
  44.2 0.1 select_reduce_fusion
  44.3 0.1 copy.10.firsts_ref
  44.4 0.0 copy-done.2
  44.5 0.1 dynamic_slice.3.slopes_ref
  44.5 3.5 %collective-permute-start.1 = (bf16[1024,512]{1,0:T(8,128)(2,1)S(1)}, bf16[1024,512]{1,0:T(8,128)(2,1)}, u32[]{:S(2)}, u32[]{:S(2)}) collective-permute-start(bf16[1024,512]{1,0:T(8,128)(2,1)S(1)} %bitcast.7), channel_id=1, source_target_pairs={{0,8},{1,9},{2,10},{3,11},{4,12},{5,13},{6,14},{7,15},{8,16},{9,17... | collective-permute-start | bytes 3145736 | tf_op jit(solution)/shard_map/ppermute | solution.py:458
  48.0 0.2 select_reduce_fusion.1
  48.2 11.2 %all-to-all-done = bf16[8,128,512]{2,1,0:T(8,128)(2,1)S(1)} async-done(((bf16[8,128,512]{2,1,0:T(8,128)(2,1)}), bf16[8,128,512]{2,1,0:T(8,128)(2,1)S(1)}, u32[]{:S(2)}, u32[]{:S(2)}) %all-to-all-start) | async-done | bytes 1048608 | tf_op jit(solution)/shard_map/all_to_all | solution.py:446
  59.5 0.0 collective-permute-done.halo_hbm
  59.5 6.7 %shard_map.57 = bf16[1024,256]{1,0:T(8,128)(2,1)S(1)} custom-call(s32[4]{0:T(128)S(1)} %fusion.tiles_ref, f32[4]{0:T(128)S(1)} %dynamic_slice.3.slopes_ref, s32[128,1]{1,0:T(8,128)S(1)} %copy.10.firsts_ref, bf16[1024,512]{1,0:T(8,128)(2,1)S(1)} %bitcast.10, bf16[1024,512]{1,0:T(8,128)(2,1)S(1)} %bitcast.15, bf16[1024,512]{1,0:T(8,128)(2,1)} %collective-permute-done.halo_hbm), custom_call_target="tpu_custom_call" | custom-call | flops 1342177280 | bytes 3145728 | tf_op jit(solution)/shard_map/pallas_call | solution.py:188
  66.1 0.0 copy-start
  66.1 0.8 copy-done
  66.9 3.5 %all-to-all-start.2 = ((bf16[8,128,256]{2,1,0:T(8,128)(2,1)}), bf16[8,128,256]{2,1,0:T(8,128)(2,1)S(1)}, u32[]{:S(2)}, u32[]{:S(2)}) async-start(bf16[8,128,256]{2,1,0:T(8,128)(2,1)} %bitcast.16), calls=%async_computation.2 | async-start | bytes 1048576 | tf_op jit(solution)/shard_map/all_to_all | solution.py:485
  70.4 3.9 %shard_map.59.part_ref = f32[2,144,1024]{2,1,0:T(8,128)S(1)} custom-call(s32[4]{0:T(128)S(1)} %fusion.tiles_ref, f32[4]{0:T(128)S(1)} %dynamic_slice.3.slopes_ref, s32[128,1]{1,0:T(8,128)S(1)} %copy.10.firsts_ref, bf16[1024,512]{1,0:T(8,128)(2,1)S(1)} %bitcast.11, bf16[1024,512]{1,0:T(8,128)(2,1)S(1)} %bitcast.8, bf16[1024,512]{1,0:T(8,128)(2,1)S(1)} %bitcast.9), custom_call_target="tpu_custom_call" | custom-call | flops 671088640 | bytes 2621440 | tf_op jit(solution)/shard_map/pallas_call | solution.py:284
  74.3 4.3 %collective-permute-done.1.halo_hbm = bf16[1024,512]{1,0:T(8,128)(2,1)} collective-permute-done((bf16[1024,512]{1,0:T(8,128)(2,1)S(1)}, bf16[1024,512]{1,0:T(8,128)(2,1)}, u32[]{:S(2)}, u32[]{:S(2)}) %collective-permute-start.1) | collective-permute-done | bytes 1048608 | tf_op jit(solution)/shard_map/ppermute | solution.py:458
  78.6 4.5 %shard_map.60 = bf16[1024,256]{1,0:T(8,128)(2,1)S(1)} custom-call(s32[4]{0:T(128)S(1)} %fusion.tiles_ref, f32[4]{0:T(128)S(1)} %dynamic_slice.3.slopes_ref, s32[128,1]{1,0:T(8,128)S(1)} %copy.10.firsts_ref, bf16[1024,512]{1,0:T(8,128)(2,1)S(1)} %bitcast.12, f32[2,144,1024]{2,1,0:T(8,128)S(1)} %shard_map.59.part_ref, ...), custom_call_target="tpu_custom_call" | custom-call | flops 671088640 | bytes 2621440 | tf_op jit(solution)/shard_map/pallas_call | solution.py:397
  83.1 0.0 all-to-all-done.2.earlier_ref.refs_0_
  83.1 13.9 %all_to_all.25.refs_1_ = bf16[8,128,256]{2,1,0:T(8,128)(2,1)S(1)} all-to-all(bf16[8,128,256]{2,1,0:T(8,128)(2,1)S(1)} %shard_map.61), channel_id=1, replica_groups={{0,1,2,3,4,5,6,7},{8,9,10,11,12,13,14,15},{16,17,18,19,20,21,22,23},{24..., dimensions={0} | all-to-all | bytes 1048576 | tf_op jit(solution)/shard_map/all_to_all | solution.py:485
  97.1 1.1 %shard_map.62 = bf16[128,4096]{1,0:T(8,128)(2,1)} custom-call(bf16[8,128,256]{2,1,0:T(8,128)(2,1)S(1)} %all-to-all-done.2.earlier_ref.refs_0_, bf16[8,128,256]{2,1,0:T(8,128)(2,1)S(1)} %all_to_all.25.refs_1_), custom_call_target="tpu_custom_call" | custom-call | tf_op jit(solution)/shard_map/pallas_call | solution.py:88
  (5 shorter events, 0.0 us)
Async XLA Ops:
  2.1 19.7 %all-to-all-start.1 = ((bf16[8,128,512]{2,1,0:T(8,128)(2,1)}), bf16[8,128,512]{2,1,0:T(8,128)(2,1)S(1)}, u32[]{:S(2)}, u32[]{:S(2)}) async-start(bf16[8,128,512]{2,1,0:T(8,128)(2,1)} %shard_map.56), calls=%async_computation.1 | async-start | bytes 2097152 | tf_op jit(solution)/shard_map/all_to_all | solution.py:446
  21.8 18.8 %all-to-all-start.3 = ((bf16[8,128,512]{2,1,0:T(8,128)(2,1)}), bf16[8,128,512]{2,1,0:T(8,128)(2,1)S(1)}, u32[]{:S(2)}, u32[]{:S(2)}) async-start(bf16[8,128,512]{2,1,0:T(8,128)(2,1)} %shard_map.58), calls=%async_computation.3 | async-start | bytes 2097152 | tf_op jit(solution)/shard_map/all_to_all | solution.py:446
  25.3 34.1 %collective-permute-start = (bf16[1024,512]{1,0:T(8,128)(2,1)S(1)}, bf16[1024,512]{1,0:T(8,128)(2,1)}, u32[]{:S(2)}, u32[]{:S(2)}) collective-permute-start(bf16[1024,512]{1,0:T(8,128)(2,1)S(1)} %bitcast.14), channel_id=1, source_target_pairs={{0,8},{1,9},{2,10},{3,11},{4,12},{5,13},{6,14},{7,15},{8,16},{9,17... | collective-permute-start | bytes 3145736 | tf_op jit(solution)/shard_map/ppermute | solution.py:458
  30.9 13.2 %copy-start.1 = (s32[128]{0:T(128)S(1)}, s32[128]{0:T(128)}, u32[]{:S(2)}) copy-start(s32[128]{0:T(128)} %param.8) | copy-start | bytes 1540
  31.0 13.5 %copy-start.2 = (f32[32]{0:T(128)S(1)}, f32[32]{0:T(128)}, u32[]{:S(2)}) copy-start(f32[32]{0:T(128)} %param.9) | copy-start | bytes 388
  40.6 18.8 %all-to-all-start = ((bf16[8,128,512]{2,1,0:T(8,128)(2,1)}), bf16[8,128,512]{2,1,0:T(8,128)(2,1)S(1)}, u32[]{:S(2)}, u32[]{:S(2)}) async-start(bf16[8,128,512]{2,1,0:T(8,128)(2,1)} %shard_map.55), calls=%async_computation | async-start | bytes 2097152 | tf_op jit(solution)/shard_map/all_to_all | solution.py:446
  44.5 34.1 %collective-permute-start.1 = (bf16[1024,512]{1,0:T(8,128)(2,1)S(1)}, bf16[1024,512]{1,0:T(8,128)(2,1)}, u32[]{:S(2)}, u32[]{:S(2)}) collective-permute-start(bf16[1024,512]{1,0:T(8,128)(2,1)S(1)} %bitcast.7), channel_id=1, source_target_pairs={{0,8},{1,9},{2,10},{3,11},{4,12},{5,13},{6,14},{7,15},{8,16},{9,17... | collective-permute-start | bytes 3145736 | tf_op jit(solution)/shard_map/ppermute | solution.py:458
  66.1 0.8 copy-start
  66.9 16.2 %all-to-all-start.2 = ((bf16[8,128,256]{2,1,0:T(8,128)(2,1)}), bf16[8,128,256]{2,1,0:T(8,128)(2,1)S(1)}, u32[]{:S(2)}, u32[]{:S(2)}) async-start(bf16[8,128,256]{2,1,0:T(8,128)(2,1)} %bitcast.16), calls=%async_computation.2 | async-start | bytes 1048576 | tf_op jit(solution)/shard_map/all_to_all | solution.py:485

commit v4 on v3

--- a/solution.py
+++ b/solution.py
@@ -95,8 +95,8 @@
 
 
 def attend_kernel(
-    inv_root, first, q_place, tiles_ref, slopes_ref, firsts_ref, q_ref, own_ref, halo_hbm,
-    out_ref, key_win, value_win, stage, sems,
+    inv_root, first, q_place, tiles_ref, slopes_ref, firsts_ref, q_ref, own_ref, halo_ref,
+    out_ref, key_win, value_win,
 ):
     span = q_ref.shape[0]
     heads = out_ref.shape[1] // 128
@@ -104,21 +104,13 @@
     most = tiles + 1
     wide = heads * 128
     before, mine = pl.ds(0, span), pl.ds(span, span)
-    copies = [
-        pltpu.make_async_copy(halo_hbm.at[:, pl.ds(wide, wide)], stage, sems.at[0]),
-        pltpu.make_async_copy(halo_hbm.at[:, pl.ds(0, wide)], key_win.at[before, :], sems.at[1]),
-    ]
-    for copy in copies:
-        copy.start()
+    key_win[before, :] = halo_ref[:, :wide]
     key_win[mine, :] = own_ref[:, :wide]
     for head in range(heads):
         columns = slice(head * 128, (head + 1) * 128)
         value_win[head, 128:, :] = jnp.ones((16, 2 * span), jnp.bfloat16)
         value_win[head, :128, mine] = own_ref[:, wide + head * 128 : wide + (head + 1) * 128].T
-    copies[0].wait()
-    for head in range(heads):
-        value_win[head, :128, before] = stage[:, head * 128 : (head + 1) * 128].T
-    copies[1].wait()
+        value_win[head, :128, before] = halo_ref[:, wide + head * 128 : wide + (head + 1) * 128].T
     firsts = firsts_ref[...]
 
     def one_tile(tile, _):
@@ -188,13 +180,11 @@
     return pl.pallas_call(
         functools.partial(attend_kernel, 1.0 / math.sqrt(128), first, q_place),
         out_shape=jax.ShapeDtypeStruct((span, heads * 128), jnp.bfloat16),
-        in_specs=[smem, smem, vmem, vmem, vmem, pl.BlockSpec(memory_space=pltpu.HBM)],
+        in_specs=[smem, smem, vmem, vmem, vmem, vmem],
         out_specs=vmem,
         scratch_shapes=[
             pltpu.VMEM((2 * span, heads * 128), jnp.bfloat16),
             pltpu.VMEM((heads, 144, 2 * span), jnp.bfloat16),
-            pltpu.VMEM((span, heads * 128), jnp.bfloat16),
-            pltpu.SemaphoreType.DMA((2,)),
         ],
         compiler_params=pltpu.CompilerParams(vmem_limit_bytes=32 << 20),
         cost_estimate=pl.CostEstimate(
@@ -297,25 +287,16 @@
 
 
 def halo_kernel(
-    inv_root, first, q_place, tiles_ref, slopes_ref, firsts_ref, q_ref, part_ref, halo_hbm,
-    out_ref, key_win, value_win, stage, sems,
+    inv_root, first, q_place, tiles_ref, slopes_ref, firsts_ref, q_ref, part_ref, halo_ref,
+    out_ref, value_win,
 ):
     span = q_ref.shape[0]
     heads = part_ref.shape[0]
     tiles = span // TILE
     wide = heads * 128
-    copies = [
-        pltpu.make_async_copy(halo_hbm.at[:, pl.ds(wide, wide)], stage, sems.at[0]),
-        pltpu.make_async_copy(halo_hbm.at[:, pl.ds(0, wide)], key_win, sems.at[1]),
-    ]
-    for copy in copies:
-        copy.start()
     for head in range(heads):
         value_win[head, 128:, :] = jnp.ones((16, span), jnp.bfloat16)
-    copies[0].wait()
-    for head in range(heads):
-        value_win[head, :128, :] = stage[:, head * 128 : (head + 1) * 128].T
-    copies[1].wait()
+        value_win[head, :128, :] = halo_ref[:, wide + head * 128 : wide + (head + 1) * 128].T
     firsts = firsts_ref[...]
 
     def one_tile(tile, _):
@@ -352,7 +333,7 @@
                 for head in range(heads):
                     all_scores.append(
                         lax.dot_general(
-                            key_win[base:, head * 128 : (head + 1) * 128],
+                            halo_ref[base:, head * 128 : (head + 1) * 128],
                             q_ref[pl.ds(row, TILE), pl.ds((q_place + head) * 128, 128)],
                             (((1,), (1,)), ((), ())),
                             preferred_element_type=jnp.float32,
@@ -397,13 +378,10 @@
     return pl.pallas_call(
         functools.partial(halo_kernel, 1.0 / math.sqrt(128), first, q_place),
         out_shape=jax.ShapeDtypeStruct((span, heads * 128), jnp.bfloat16),
-        in_specs=[smem, smem, vmem, vmem, vmem, pl.BlockSpec(memory_space=pltpu.HBM)],
+        in_specs=[smem, smem, vmem, vmem, vmem, vmem],
         out_specs=vmem,
         scratch_shapes=[
-            pltpu.VMEM((span, heads * 128), jnp.bfloat16),
             pltpu.VMEM((heads, 144, span), jnp.bfloat16),
-            pltpu.VMEM((span, heads * 128), jnp.bfloat16),
-            pltpu.SemaphoreType.DMA((2,)),
         ],
         compiler_params=pltpu.CompilerParams(vmem_limit_bytes=32 << 20),
         cost_estimate=pl.CostEstimate(

time: 99.1 us -> 98.9 us (level)
  the two profiles are of different devices: /device:TPU:256 before, /device:TPU:1 now
where the time goes in v4:
time: 98.9 us; the launch traced here: 98.3 us
  waiting for transfers between devices  38.3 us (39%)
  starting transfers between devices  26.4 us (27%)
  Pallas kernels  19.6 us (20%)
  blocking collectives  12.6 us (13%)
  local copies, waits for them, and re-layouts  0.99 us (1%)
    all_to_all x3, waiting for transfers between devices, exchange(): got = lax.all_to_all(value, AXES, 0, 0, axis_index_groups=index_groups)  35.6 us
    all_to_all x3, starting transfers between devices, exchange(): got = lax.all_to_all(value, AXES, 0, 0, axis_index_groups=index_groups)  18.1 us
    all_to_all x1, blocking collectives, per_device(): lax.all_to_all(sent, AXES, 0, 0, axis_index_groups=index_groups)  12.6 us
    pallas_call x3, Pallas kernels, pack(): pl.pallas_call(functools.partial(pack_kernel, pieces, count), out_shape=j...  6.33 us
    pallas_call x1, Pallas kernels, attend(): pl.pallas_call(functools.partial(attend_kernel, 1.0 / math.sqrt(128), fir...  5.59 us
    ppermute x2, starting transfers between devices, per_device(): halo.append(lax.ppermute(got[:, :2 * kv * 128], AXES, onward))  4.57 us
    pallas_call x1, Pallas kernels, attend_own(): pl.pallas_call(functools.partial(own_kernel, 1.0 / math.sqrt(128), first,...  4.34 us
    all_to_all x1, starting transfers between devices, per_device(): lax.all_to_all(sent, AXES, 0, 0, axis_index_groups=index_groups)  3.78 us
  transfers between devices with their start and end apart: 6, of which 4 were waited for; matrix products, arithmetic and copies ran while one was open for 1% of the time, Pallas kernels for 17%

profile of v4, /device:TPU:1, one launch (start us, length us, event | category | flops | bytes accessed | tf_op | source)
XLA Modules:
  0.0 98.3 jit_solution(4835148904578270543)
XLA Ops:
  0.0 2.1 %shard_map.56 = bf16[8,128,512]{2,1,0:T(8,128)(2,1)} custom-call(bf16[128,4096]{1,0:T(8,128)(2,1)} %refs_0_.5, bf16[128,4096]{1,0:T(8,128)(2,1)} %refs_1_.3), custom_call_target="tpu_custom_call" | custom-call | bytes 2097152 | tf_op jit(solution)/shard_map/pallas_call | solution.py:58
  2.1 10.4 %all-to-all-start.1 = ((bf16[8,128,512]{2,1,0:T(8,128)(2,1)}), bf16[8,128,512]{2,1,0:T(8,128)(2,1)S(1)}, u32[]{:S(2)}, u32[]{:S(2)}) async-start(bf16[8,128,512]{2,1,0:T(8,128)(2,1)} %shard_map.56), calls=%async_computation.1 | async-start | bytes 2097152 | tf_op jit(solution)/shard_map/all_to_all | solution.py:424
  12.5 2.1 %shard_map.58 = bf16[8,128,512]{2,1,0:T(8,128)(2,1)} custom-call(bf16[128,4096]{1,0:T(8,128)(2,1)} %refs_0_.5, bf16[128,4096]{1,0:T(8,128)(2,1)} %refs_1_.3), custom_call_target="tpu_custom_call" | custom-call | bytes 2097152 | tf_op jit(solution)/shard_map/pallas_call | solution.py:58
  14.6 12.9 %all-to-all-done.1 = bf16[8,128,512]{2,1,0:T(8,128)(2,1)S(1)} async-done(((bf16[8,128,512]{2,1,0:T(8,128)(2,1)}), bf16[8,128,512]{2,1,0:T(8,128)(2,1)S(1)}, u32[]{:S(2)}, u32[]{:S(2)}) %all-to-all-start.1) | async-done | bytes 1048608 | tf_op jit(solution)/shard_map/all_to_all | solution.py:424
  27.5 3.8 %all-to-all-start.3 = ((bf16[8,128,512]{2,1,0:T(8,128)(2,1)}), bf16[8,128,512]{2,1,0:T(8,128)(2,1)S(1)}, u32[]{:S(2)}, u32[]{:S(2)}) async-start(bf16[8,128,512]{2,1,0:T(8,128)(2,1)} %shard_map.58), calls=%async_computation.3 | async-start | bytes 2097152 | tf_op jit(solution)/shard_map/all_to_all | solution.py:424
  31.3 2.3 %collective-permute-start = (bf16[1024,512]{1,0:T(8,128)(2,1)S(1)}, bf16[1024,512]{1,0:T(8,128)(2,1)}, u32[]{:S(2)}, u32[]{:S(2)}) collective-permute-start(bf16[1024,512]{1,0:T(8,128)(2,1)S(1)} %bitcast.14), channel_id=1, source_target_pairs={{0,8},{1,9},{2,10},{3,11},{4,12},{5,13},{6,14},{7,15},{8,16},{9,17... | collective-permute-start | bytes 3145736 | tf_op jit(solution)/shard_map/ppermute | solution.py:436
  33.6 2.1 %shard_map.55 = bf16[8,128,512]{2,1,0:T(8,128)(2,1)} custom-call(bf16[128,4096]{1,0:T(8,128)(2,1)} %refs_0_.3), custom_call_target="tpu_custom_call" | custom-call | bytes 2097152 | tf_op jit(solution)/shard_map/pallas_call | solution.py:58
  35.7 0.0 copy-start.1
  35.7 0.0 copy-start.2
  35.7 10.6 %all-to-all-done.3 = bf16[8,128,512]{2,1,0:T(8,128)(2,1)S(1)} async-done(((bf16[8,128,512]{2,1,0:T(8,128)(2,1)}), bf16[8,128,512]{2,1,0:T(8,128)(2,1)S(1)}, u32[]{:S(2)}, u32[]{:S(2)}) %all-to-all-start.3) | async-done | bytes 1048608 | tf_op jit(solution)/shard_map/all_to_all | solution.py:424
  46.3 3.8 %all-to-all-start = ((bf16[8,128,512]{2,1,0:T(8,128)(2,1)}), bf16[8,128,512]{2,1,0:T(8,128)(2,1)S(1)}, u32[]{:S(2)}, u32[]{:S(2)}) async-start(bf16[8,128,512]{2,1,0:T(8,128)(2,1)} %shard_map.55), calls=%async_computation | async-start | bytes 2097152 | tf_op jit(solution)/shard_map/all_to_all | solution.py:424
  50.2 0.0 copy-done.1
  50.2 0.1 select_reduce_fusion
  50.3 0.1 copy.10.firsts_ref
  50.4 0.0 copy-done.2
  50.4 0.1 dynamic_slice.3.slopes_ref
  50.5 2.3 %collective-permute-start.1 = (bf16[1024,512]{1,0:T(8,128)(2,1)S(1)}, bf16[1024,512]{1,0:T(8,128)(2,1)}, u32[]{:S(2)}, u32[]{:S(2)}) collective-permute-start(bf16[1024,512]{1,0:T(8,128)(2,1)S(1)} %bitcast.7), channel_id=1, source_target_pairs={{0,8},{1,9},{2,10},{3,11},{4,12},{5,13},{6,14},{7,15},{8,16},{9,17... | collective-permute-start | bytes 3145736 | tf_op jit(solution)/shard_map/ppermute | solution.py:436
  52.8 0.2 select_reduce_fusion.1
  53.0 12.1 %all-to-all-done = bf16[8,128,512]{2,1,0:T(8,128)(2,1)S(1)} async-done(((bf16[8,128,512]{2,1,0:T(8,128)(2,1)}), bf16[8,128,512]{2,1,0:T(8,128)(2,1)S(1)}, u32[]{:S(2)}, u32[]{:S(2)}) %all-to-all-start) | async-done | bytes 1048608 | tf_op jit(solution)/shard_map/all_to_all | solution.py:424
  65.2 0.0 collective-permute-done.halo_ref
  65.2 5.6 %shard_map.57 = bf16[1024,256]{1,0:T(8,128)(2,1)S(1)} custom-call(s32[4]{0:T(128)S(1)} %fusion.tiles_ref, f32[4]{0:T(128)S(1)} %dynamic_slice.3.slopes_ref, s32[128,1]{1,0:T(8,128)S(1)} %copy.10.firsts_ref, bf16[1024,512]{1,0:T(8,128)(2,1)S(1)} %bitcast.10, bf16[1024,512]{1,0:T(8,128)(2,1)S(1)} %bitcast.15, bf16[1024,512]{1,0:T(8,128)(2,1)} %collective-permute-done.halo_ref), custom_call_target="tpu_custom_call" | custom-call | flops 1342177280 | bytes 3145728 | tf_op jit(solution)/shard_map/pallas_call | solution.py:180
  70.8 0.0 copy-start
  70.8 0.8 copy-done
  71.6 3.8 %all-to-all-start.2 = ((bf16[8,128,256]{2,1,0:T(8,128)(2,1)}), bf16[8,128,256]{2,1,0:T(8,128)(2,1)S(1)}, u32[]{:S(2)}, u32[]{:S(2)}) async-start(bf16[8,128,256]{2,1,0:T(8,128)(2,1)} %bitcast.16), calls=%async_computation.2 | async-start | bytes 1048576 | tf_op jit(solution)/shard_map/all_to_all | solution.py:463
  75.3 4.3 %shard_map.59.part_ref = f32[2,144,1024]{2,1,0:T(8,128)S(1)} custom-call(s32[4]{0:T(128)S(1)} %fusion.tiles_ref, f32[4]{0:T(128)S(1)} %dynamic_slice.3.slopes_ref, s32[128,1]{1,0:T(8,128)S(1)} %copy.10.firsts_ref, bf16[1024,512]{1,0:T(8,128)(2,1)S(1)} %bitcast.11, bf16[1024,512]{1,0:T(8,128)(2,1)S(1)} %bitcast.8, bf16[1024,512]{1,0:T(8,128)(2,1)S(1)} %bitcast.9), custom_call_target="tpu_custom_call" | custom-call | flops 671088640 | bytes 2621440 | tf_op jit(solution)/shard_map/pallas_call | solution.py:274
  79.7 0.0 collective-permute-done.1.halo_ref
  79.7 2.3 %shard_map.60 = bf16[1024,256]{1,0:T(8,128)(2,1)S(1)} custom-call(s32[4]{0:T(128)S(1)} %fusion.tiles_ref, f32[4]{0:T(128)S(1)} %dynamic_slice.3.slopes_ref, s32[128,1]{1,0:T(8,128)S(1)} %copy.10.firsts_ref, bf16[1024,512]{1,0:T(8,128)(2,1)S(1)} %bitcast.12, f32[2,144,1024]{2,1,0:T(8,128)S(1)} %shard_map.59.part_ref, ...), custom_call_target="tpu_custom_call" | custom-call | flops 671088640 | bytes 2621440 | tf_op jit(solution)/shard_map/pallas_call | solution.py:378
  82.0 2.7 %all-to-all-done.2.earlier_ref.refs_0_ = bf16[8,128,256]{2,1,0:T(8,128)(2,1)S(1)} async-done(((bf16[8,128,256]{2,1,0:T(8,128)(2,1)}), bf16[8,128,256]{2,1,0:T(8,128)(2,1)S(1)}, u32[]{:S(2)}, u32[]{:S(2)}) %all-to-all-start.2) | async-done | bytes 524320 | tf_op jit(solution)/shard_map/all_to_all | solution.py:463
  84.7 12.6 %all_to_all.25.refs_1_ = bf16[8,128,256]{2,1,0:T(8,128)(2,1)S(1)} all-to-all(bf16[8,128,256]{2,1,0:T(8,128)(2,1)S(1)} %shard_map.61), channel_id=1, replica_groups={{0,1,2,3,4,5,6,7},{8,9,10,11,12,13,14,15},{16,17,18,19,20,21,22,23},{24..., dimensions={0} | all-to-all | bytes 1048576 | tf_op jit(solution)/shard_map/all_to_all | solution.py:463
  97.3 1.1 %shard_map.62 = bf16[128,4096]{1,0:T(8,128)(2,1)} custom-call(bf16[8,128,256]{2,1,0:T(8,128)(2,1)S(1)} %all-to-all-done.2.earlier_ref.refs_0_, bf16[8,128,256]{2,1,0:T(8,128)(2,1)S(1)} %all_to_all.25.refs_1_), custom_call_target="tpu_custom_call" | custom-call | tf_op jit(solution)/shard_map/pallas_call | solution.py:88
  (5 shorter events, 0.0 us)
Async XLA Ops:
  2.1 25.4 %all-to-all-start.1 = ((bf16[8,128,512]{2,1,0:T(8,128)(2,1)}), bf16[8,128,512]{2,1,0:T(8,128)(2,1)S(1)}, u32[]{:S(2)}, u32[]{:S(2)}) async-start(bf16[8,128,512]{2,1,0:T(8,128)(2,1)} %shard_map.56), calls=%async_computation.1 | async-start | bytes 2097152 | tf_op jit(solution)/shard_map/all_to_all | solution.py:424
  27.5 18.8 %all-to-all-start.3 = ((bf16[8,128,512]{2,1,0:T(8,128)(2,1)}), bf16[8,128,512]{2,1,0:T(8,128)(2,1)S(1)}, u32[]{:S(2)}, u32[]{:S(2)}) async-start(bf16[8,128,512]{2,1,0:T(8,128)(2,1)} %shard_map.58), calls=%async_computation.3 | async-start | bytes 2097152 | tf_op jit(solution)/shard_map/all_to_all | solution.py:424
  31.3 33.8 %collective-permute-start = (bf16[1024,512]{1,0:T(8,128)(2,1)S(1)}, bf16[1024,512]{1,0:T(8,128)(2,1)}, u32[]{:S(2)}, u32[]{:S(2)}) collective-permute-start(bf16[1024,512]{1,0:T(8,128)(2,1)S(1)} %bitcast.14), channel_id=1, source_target_pairs={{0,8},{1,9},{2,10},{3,11},{4,12},{5,13},{6,14},{7,15},{8,16},{9,17... | collective-permute-start | bytes 3145736 | tf_op jit(solution)/shard_map/ppermute | solution.py:436
  35.7 14.5 %copy-start.1 = (s32[128]{0:T(128)S(1)}, s32[128]{0:T(128)}, u32[]{:S(2)}) copy-start(s32[128]{0:T(128)} %param.8) | copy-start | bytes 1540
  35.7 14.7 %copy-start.2 = (f32[32]{0:T(128)S(1)}, f32[32]{0:T(128)}, u32[]{:S(2)}) copy-start(f32[32]{0:T(128)} %param.9) | copy-start | bytes 388
  46.3 18.8 %all-to-all-start = ((bf16[8,128,512]{2,1,0:T(8,128)(2,1)}), bf16[8,128,512]{2,1,0:T(8,128)(2,1)S(1)}, u32[]{:S(2)}, u32[]{:S(2)}) async-start(bf16[8,128,512]{2,1,0:T(8,128)(2,1)} %shard_map.55), calls=%async_computation | async-start | bytes 2097152 | tf_op jit(solution)/shard_map/all_to_all | solution.py:424
  50.5 29.2 %collective-permute-start.1 = (bf16[1024,512]{1,0:T(8,128)(2,1)S(1)}, bf16[1024,512]{1,0:T(8,128)(2,1)}, u32[]{:S(2)}, u32[]{:S(2)}) collective-permute-start(bf16[1024,512]{1,0:T(8,128)(2,1)S(1)} %bitcast.7), channel_id=1, source_target_pairs={{0,8},{1,9},{2,10},{3,11},{4,12},{5,13},{6,14},{7,15},{8,16},{9,17... | collective-permute-start | bytes 3145736 | tf_op jit(solution)/shard_map/ppermute | solution.py:436
  70.8 0.8 copy-start
  71.6 13.2 %all-to-all-start.2 = ((bf16[8,128,256]{2,1,0:T(8,128)(2,1)}), bf16[8,128,256]{2,1,0:T(8,128)(2,1)S(1)}, u32[]{:S(2)}, u32[]{:S(2)}) async-start(bf16[8,128,256]{2,1,0:T(8,128)(2,1)} %bitcast.16), calls=%async_computation.2 | async-start | bytes 1048576 | tf_op jit(solution)/shard_map/all_to_all | solution.py:463
